TPU v7x, 32 devices: a whole 2x2x4 slice. The times are simulated.
32 devices in a mesh: dp: 4 (over z), ctx: 8 (over y, x, core).
Axes of the slice: x: 2, y: 2, z: 4, core: 2. Of those that a mesh axis runs over, the one named last changes fastest.
Arguments:
- tokens: bfloat16 [8, 2048, 768], P('dp', 'ctx'), may hold values from -6 to 6
- segments: int32 [8, 2048], P('dp', 'ctx'), may hold values from 0 to 15, as said below
- positions: int32 [8, 2048], P('dp', 'ctx'), may hold values from 0 to 6141, as said below
- gain_attn: bfloat16 [768], P(('dp', 'ctx')), may hold values from 0.099609375 to 1.8984375
- shift_attn: bfloat16 [768], P(('dp', 'ctx')), may hold values from -4 to 4
- gain_mlp: bfloat16 [768], P(('dp', 'ctx')), may hold values from 0.099609375 to 1.8984375
- shift_mlp: bfloat16 [768], P(('dp', 'ctx')), may hold values from -4 to 4
- qkv_weight: bfloat16 [768, 2304], P(('dp', 'ctx')), may hold values from -0.21875 to 0.21875
- query_bias: bfloat16 [768], P(('dp', 'ctx')), may hold values from -4 to 4
- key_bias: bfloat16 [768], P(('dp', 'ctx')), may hold values from -6 to 6
- value_bias: bfloat16 [768], P(('dp', 'ctx')), may hold values from -1.5 to 1.5
- dense_weight: bfloat16 [768, 768], P(('dp', 'ctx')), may hold values from -0.875 to 0.875
- expand_weight: bfloat16 [768, 3072], P(('dp', 'ctx')), may hold values from -0.21875 to 0.21875
- expand_bias: bfloat16 [3072], P(('dp', 'ctx')), may hold values from -4 to 4
- contract_weight: bfloat16 [3072, 768], P(('dp', 'ctx')), may hold values from -0.109375 to 0.109375
- output_bias: bfloat16 [768], P(('dp', 'ctx')), may hold values from -4 to 4
- cotangent: bfloat16 [8, 2048, 768], P('dp', 'ctx'), may hold values from -6 to 6
Outputs:
- output: bfloat16 [8, 2048, 768], P('dp', 'ctx')
- input_grad: bfloat16 [8, 2048, 768], P('dp', 'ctx')
- grad_gain_attn: float32 [768], P(('dp', 'ctx'))
- grad_shift_attn: float32 [768], P(('dp', 'ctx'))
- grad_gain_mlp: float32 [768], P(('dp', 'ctx'))
- grad_shift_mlp: float32 [768], P(('dp', 'ctx'))
- grad_qkv_weight: float32 [768, 2304], P(('dp', 'ctx'))
- grad_query_bias: float32 [768], P(('dp', 'ctx'))
- grad_key_bias: float32 [768], P(('dp', 'ctx'))
- grad_value_bias: float32 [768], P(('dp', 'ctx'))
- grad_dense_weight: float32 [768, 768], P(('dp', 'ctx'))
- grad_expand_weight: float32 [768, 3072], P(('dp', 'ctx'))
- grad_expand_bias: float32 [3072], P(('dp', 'ctx'))
- grad_contract_weight: float32 [3072, 768], P(('dp', 'ctx'))
- grad_output_bias: float32 [768], P(('dp', 'ctx'))
Inputs may be any that keep to these rules, and one draw needn't show every extreme that they name: `segments`: along each sequence the document number is 0 at the first token and rises by 0 or 1 from one token to the next; a sequence holds at most 16 documents; among the 2 sequences of each index of dp, one is a single document and another holds exactly 16. `positions`: 0 at the first token of each document, rising by 1 to 3 from one token to the next within a document; in the single-document sequence of each index of dp it rises by exactly 3.
All inputs are finite; a program needn't handle non-finite values.
Results may differ from a plain program's by a relative error of at most 0.03.
Values may be sent and summed in bfloat16 or wider, within the bound.
No kernel may reach another device: no remote copies, remote signals or barrier semaphores. Data moves between devices by JAX's collectives and lax.ppermute only.
A program may use at most 192 MiB of HBM per device.

v0:
```python
import math

import jax
import jax.numpy as jnp
from jax import lax
from jax.sharding import PartitionSpec as P

HEAD_DIM = 64
ROT_DIMS = 16


NEG_BIG = -1e30
EPSILON = 1e-05


def from_behind(value, axis, by):
    size = lax.axis_size(axis)
    pairs = [(i, i + by) for i in range(size) if 0 <= i + by < size]
    return lax.ppermute(value, axis, pairs)


def shifted(value, axis, by):
    size = lax.axis_size(axis)
    return lax.ppermute(value, axis, [(i, (i + by) % size) for i in range(size)])


def normalize(values, gain_vec, shift_vec):
    centre = values - jnp.mean(values, axis=-1, keepdims=True)
    spread = jnp.mean(centre * centre, axis=-1, keepdims=True)
    return centre * lax.rsqrt(spread + EPSILON) * gain_vec + shift_vec


def angles(positions):
    ladder = jnp.arange(ROT_DIMS // 2).astype(jnp.float32)
    inverse = jnp.exp(ladder * (-2.0 * math.log(10000.0) / ROT_DIMS))
    phase_angle = positions.astype(jnp.float32)[..., None] * inverse
    return (jnp.cos(phase_angle)[..., None, :], jnp.sin(phase_angle)[..., None, :])


def rotate(field_in, cosine, sine_part):
    half_dims = ROT_DIMS // 2
    lower_half = field_in[..., :half_dims]
    upper_half = field_in[..., half_dims:ROT_DIMS]
    remainder = field_in[..., ROT_DIMS:]
    return jnp.concatenate(
        [
            lower_half * cosine - upper_half * sine_part,
            upper_half * cosine + lower_half * sine_part,
            remainder,
        ],
        axis=-1,
    )


def exact_gelu(pre_act):
    return jax.nn.gelu(pre_act, approximate=False)


def contract_last(left_side, right_side):
    return lax.dot_general(
        left_side, right_side, (((1,), (1,)), ((), ())), preferred_element_type=jnp.float32
    )


def visible(query_seg, query_start, key_seg, key_start):
    query_index = query_start + jnp.arange(query_seg.shape[1])
    key_index = key_start + jnp.arange(key_seg.shape[1])
    allowed = (key_index[None, None, :] <= query_index[None, :, None]) & (
        key_seg[:, None, :] == query_seg[:, :, None]
    )
    return allowed[:, :, None, :]


def pair_grads(query_side, stats_side, query_start, key_side, key_start):
    query_rows, d_mixed, query_seg = query_side
    log_total, delta_rows = stats_side
    key_rows, value_rows, key_seg = key_side
    score_scale = 1.0 / math.sqrt(HEAD_DIM)
    allowed = visible(query_seg, query_start, key_seg, key_start)
    scores = (
        jnp.einsum("bqhd,bkhd->bqhk", query_rows, key_rows, preferred_element_type=jnp.float32)
        * score_scale
    )
    prob_rows = jnp.where(
        allowed, jnp.exp(jnp.where(allowed, scores - log_total[..., None], NEG_BIG)), 0.0
    )
    d_prob = jnp.einsum("bqhd,bkhd->bqhk", d_mixed, value_rows, preferred_element_type=jnp.float32)
    d_scores = (prob_rows * (d_prob - delta_rows[..., None])).astype(jnp.bfloat16)
    d_query = (
        jnp.einsum("bqhk,bkhd->bqhd", d_scores, key_rows, preferred_element_type=jnp.float32)
        * score_scale
    )
    d_key = (
        jnp.einsum("bqhk,bqhd->bkhd", d_scores, query_rows, preferred_element_type=jnp.float32)
        * score_scale
    )
    d_value = jnp.einsum(
        "bqhk,bqhd->bkhd",
        prob_rows.astype(jnp.bfloat16),
        d_mixed,
        preferred_element_type=jnp.float32,
    )
    return (d_query, d_key, d_value)


def per_device(
    tokens,
    segments,
    positions,
    gain_attn,
    shift_attn,
    gain_mlp,
    shift_mlp,
    qkv_weight,
    query_bias,
    key_bias,
    value_bias,
    dense_weight,
    expand_weight,
    expand_bias,
    contract_weight,
    output_bias,
    cotangent,
):
    shards = (
        gain_attn,
        shift_attn,
        gain_mlp,
        shift_mlp,
        qkv_weight,
        query_bias,
        key_bias,
        value_bias,
        dense_weight,
        expand_weight,
        expand_bias,
        contract_weight,
        output_bias,
    )
    gathered = (
        lax.all_gather(shards[0], ("dp", "ctx"), axis=0, tiled=True),
        lax.all_gather(shards[1], ("dp", "ctx"), axis=0, tiled=True),
        lax.all_gather(shards[2], ("dp", "ctx"), axis=0, tiled=True),
        lax.all_gather(shards[3], ("dp", "ctx"), axis=0, tiled=True),
        lax.all_gather(shards[4], ("dp", "ctx"), axis=0, tiled=True),
        lax.all_gather(shards[5], ("dp", "ctx"), axis=0, tiled=True),
        lax.all_gather(shards[6], ("dp", "ctx"), axis=0, tiled=True),
        lax.all_gather(shards[7], ("dp", "ctx"), axis=0, tiled=True),
        lax.all_gather(shards[8], ("dp", "ctx"), axis=0, tiled=True),
        lax.all_gather(shards[9], ("dp", "ctx"), axis=0, tiled=True),
        lax.all_gather(shards[10], ("dp", "ctx"), axis=0, tiled=True),
        lax.all_gather(shards[11], ("dp", "ctx"), axis=0, tiled=True),
        lax.all_gather(shards[12], ("dp", "ctx"), axis=0, tiled=True),
    )
    seq_count, tok_count, model_width = tokens.shape
    row_count = seq_count * tok_count
    head_count = model_width // HEAD_DIM
    heads_shape = (seq_count, tok_count, head_count, HEAD_DIM)
    flat_shape = (seq_count, tok_count, model_width)
    full_gain_attn = gathered[0].astype(jnp.float32)
    full_shift_attn = gathered[1].astype(jnp.float32)
    full_gain_mlp = gathered[2].astype(jnp.float32)
    full_shift_mlp = gathered[3].astype(jnp.float32)
    full_query_bias = gathered[5].astype(jnp.float32)
    full_key_bias = gathered[6].astype(jnp.float32)
    full_value_bias = gathered[7].astype(jnp.float32)
    full_expand_bias = gathered[10].astype(jnp.float32)
    full_output_bias = gathered[12].astype(jnp.float32)
    flat_in = tokens.reshape(row_count, model_width).astype(jnp.float32)

    def both_norms(values, gain_one, shift_one, gain_two, shift_two):
        return (normalize(values, gain_one, shift_one), normalize(values, gain_two, shift_two))

    (norm_attn, norm_mlp), norm_pull = jax.vjp(
        both_norms, flat_in, full_gain_attn, full_shift_attn, full_gain_mlp, full_shift_mlp
    )
    attn_in = norm_attn.astype(jnp.bfloat16)
    mlp_in = norm_mlp.astype(jnp.bfloat16)
    packed = jnp.dot(attn_in, gathered[4], preferred_element_type=jnp.float32)
    query_raw = (packed[:, :model_width] + full_query_bias).reshape(heads_shape)
    key_raw = (packed[:, model_width : 2 * model_width] + full_key_bias).reshape(heads_shape)
    value_rows = (
        (packed[:, 2 * model_width :] + full_value_bias).astype(jnp.bfloat16).reshape(heads_shape)
    )
    cosine, sine_part = angles(positions)

    def turn_heads(field_in):
        return rotate(field_in, cosine, sine_part)

    query_turned, query_pull = jax.vjp(turn_heads, query_raw)
    key_turned, key_pull = jax.vjp(turn_heads, key_raw)
    query_rows = query_turned.astype(jnp.bfloat16)
    key_rows = key_turned.astype(jnp.bfloat16)
    key_flat = key_rows.reshape(flat_shape)
    value_flat = value_rows.reshape(flat_shape)
    ctx_count = lax.axis_size("ctx")
    ctx_index = lax.axis_index("ctx")
    here_start = ctx_index * tok_count
    score_scale = 1.0 / math.sqrt(HEAD_DIM)
    start_max = jnp.full((seq_count, tok_count, head_count), NEG_BIG, jnp.float32)
    key_blk = lax.all_gather(key_flat, "ctx", axis=1, tiled=True)
    value_blk = lax.all_gather(value_flat, "ctx", axis=1, tiled=True)
    seg_blk = lax.all_gather(segments, "ctx", axis=1, tiled=True)
    block_len = key_blk.shape[1]
    key_blk = key_blk.reshape(seq_count, block_len, head_count, HEAD_DIM)
    value_blk = value_blk.reshape(seq_count, block_len, head_count, HEAD_DIM)
    allowed = visible(segments, here_start, seg_blk, jnp.int32(0))
    scores = (
        jnp.einsum("bqhd,bkhd->bqhk", query_rows, key_blk, preferred_element_type=jnp.float32)
        * score_scale
    )
    scores = jnp.where(allowed, scores, NEG_BIG)
    new_max = jnp.maximum(start_max, jnp.max(scores, axis=-1))
    weights = jnp.where(allowed, jnp.exp(scores - new_max[..., None]), 0.0)
    new_sum = jnp.sum(weights, axis=-1)
    new_acc = jnp.einsum(
        "bqhk,bkhd->bqhd",
        weights.astype(jnp.bfloat16),
        value_blk,
        preferred_element_type=jnp.float32,
    )
    log_total = new_max + jnp.log(new_sum)
    mixed_full = new_acc / new_sum[..., None]
    mixed_rows = mixed_full.astype(jnp.bfloat16).reshape(row_count, model_width)
    hidden_pre = jnp.dot(mlp_in, gathered[9], preferred_element_type=jnp.float32) + full_expand_bias
    hidden_act, gelu_pull = jax.vjp(exact_gelu, hidden_pre)
    hidden_rows = hidden_act.astype(jnp.bfloat16)
    result = (
        flat_in
        + jnp.dot(mixed_rows, gathered[8], preferred_element_type=jnp.float32)
        + jnp.dot(hidden_rows, gathered[11], preferred_element_type=jnp.float32)
        + full_output_bias
    )
    output = result.astype(jnp.bfloat16).reshape(flat_shape)
    regathered = (
        lax.all_gather(shards[0], ("dp", "ctx"), axis=0, tiled=True),
        lax.all_gather(shards[1], ("dp", "ctx"), axis=0, tiled=True),
        lax.all_gather(shards[2], ("dp", "ctx"), axis=0, tiled=True),
        lax.all_gather(shards[3], ("dp", "ctx"), axis=0, tiled=True),
        lax.all_gather(shards[4], ("dp", "ctx"), axis=0, tiled=True),
        lax.all_gather(shards[5], ("dp", "ctx"), axis=0, tiled=True),
        lax.all_gather(shards[6], ("dp", "ctx"), axis=0, tiled=True),
        lax.all_gather(shards[7], ("dp", "ctx"), axis=0, tiled=True),
        lax.all_gather(shards[8], ("dp", "ctx"), axis=0, tiled=True),
        lax.all_gather(shards[9], ("dp", "ctx"), axis=0, tiled=True),
        lax.all_gather(shards[10], ("dp", "ctx"), axis=0, tiled=True),
        lax.all_gather(shards[11], ("dp", "ctx"), axis=0, tiled=True),
        lax.all_gather(shards[12], ("dp", "ctx"), axis=0, tiled=True),
    )
    back_qkv = regathered[4]
    back_dense = regathered[8]
    back_expand = regathered[9]
    back_contract = regathered[11]
    grad_rows = cotangent.reshape(row_count, model_width)
    grad_full = grad_rows.astype(jnp.float32)
    d_output_bias = jnp.sum(grad_full, axis=0)
    d_contract = jnp.einsum("rf,rd->fd", hidden_rows, grad_rows, preferred_element_type=jnp.float32)
    d_hidden = contract_last(grad_rows, back_contract)
    d_hidden_pre = gelu_pull(d_hidden)[0].astype(jnp.bfloat16)
    d_expand_bias = jnp.sum(d_hidden_pre.astype(jnp.float32), axis=0)
    d_expand = jnp.einsum("rd,rf->df", mlp_in, d_hidden_pre, preferred_element_type=jnp.float32)
    d_norm_mlp = contract_last(d_hidden_pre, back_expand)
    d_dense = jnp.einsum("ri,rd->id", mixed_rows, grad_rows, preferred_element_type=jnp.float32)
    d_mixed = contract_last(grad_rows, back_dense).astype(jnp.bfloat16).reshape(heads_shape)
    delta_rows = jnp.sum(d_mixed.astype(jnp.float32) * mixed_full, axis=-1)
    query_side = (query_rows, d_mixed, segments)
    stats_side = (log_total, delta_rows)

    def carry_step(step_num, loop_state):
        key_block, grad_block, d_query_acc = loop_state
        owner_dev = (ctx_index - step_num) % ctx_count
        key_side = (
            key_block[0].reshape(heads_shape),
            key_block[1].reshape(heads_shape),
            key_block[2],
        )
        d_query_part, d_key_part, d_value_part = pair_grads(
            query_side, stats_side, here_start, key_side, owner_dev * tok_count
        )
        grad_block = (
            grad_block[0] + d_key_part.reshape(flat_shape),
            grad_block[1] + d_value_part.reshape(flat_shape),
        )
        key_block = from_behind((key_block[0], key_block[1], key_block[2]), "ctx", 1)
        grad_block = (
            shifted(grad_block[0].astype(jnp.bfloat16), "ctx", 1).astype(jnp.float32),
            shifted(grad_block[1].astype(jnp.bfloat16), "ctx", 1).astype(jnp.float32),
        )
        return (key_block, grad_block, d_query_acc + d_query_part)

    zero_flat = jnp.zeros(flat_shape, jnp.float32)
    final_state = lax.fori_loop(
        0,
        ctx_count,
        carry_step,
        (
            (key_flat, value_flat, segments),
            (zero_flat, zero_flat),
            jnp.zeros(heads_shape, jnp.float32),
        ),
    )
    d_query_sum = final_state[2]
    d_key_sum = final_state[1][0].reshape(heads_shape)
    d_value_sum = final_state[1][1].reshape(heads_shape)
    d_query_raw = query_pull(d_query_sum)[0].astype(jnp.bfloat16).reshape(row_count, model_width)
    d_key_raw = key_pull(d_key_sum)[0].astype(jnp.bfloat16).reshape(row_count, model_width)
    d_value_low = d_value_sum.astype(jnp.bfloat16).reshape(row_count, model_width)
    d_query_bias = jnp.sum(d_query_raw.astype(jnp.float32), axis=0)
    d_key_bias = jnp.sum(d_key_raw.astype(jnp.float32), axis=0)
    d_value_bias = jnp.sum(d_value_low.astype(jnp.float32), axis=0)
    d_packed = jnp.concatenate([d_query_raw, d_key_raw, d_value_low], axis=1)
    d_qkv = jnp.einsum("rd,rp->dp", attn_in, d_packed, preferred_element_type=jnp.float32)
    d_norm_attn = contract_last(d_packed, back_qkv)
    d_flat, d_gain_attn, d_shift_attn, d_gain_mlp, d_shift_mlp = norm_pull(
        (d_norm_attn, d_norm_mlp)
    )
    input_grad = (grad_full + d_flat).astype(jnp.bfloat16).reshape(flat_shape)
    owned_grads = (
        lax.psum_scatter(d_gain_attn, ("dp", "ctx"), scatter_dimension=0, tiled=True),
        lax.psum_scatter(d_shift_attn, ("dp", "ctx"), scatter_dimension=0, tiled=True),
        lax.psum_scatter(d_gain_mlp, ("dp", "ctx"), scatter_dimension=0, tiled=True),
        lax.psum_scatter(d_shift_mlp, ("dp", "ctx"), scatter_dimension=0, tiled=True),
        lax.psum_scatter(d_qkv, ("dp", "ctx"), scatter_dimension=0, tiled=True),
        lax.psum_scatter(d_query_bias, ("dp", "ctx"), scatter_dimension=0, tiled=True),
        lax.psum_scatter(d_key_bias, ("dp", "ctx"), scatter_dimension=0, tiled=True),
        lax.psum_scatter(d_value_bias, ("dp", "ctx"), scatter_dimension=0, tiled=True),
        lax.psum_scatter(d_dense, ("dp", "ctx"), scatter_dimension=0, tiled=True),
        lax.psum_scatter(d_expand, ("dp", "ctx"), scatter_dimension=0, tiled=True),
        lax.psum_scatter(d_expand_bias, ("dp", "ctx"), scatter_dimension=0, tiled=True),
        lax.psum_scatter(d_contract, ("dp", "ctx"), scatter_dimension=0, tiled=True),
        lax.psum_scatter(d_output_bias, ("dp", "ctx"), scatter_dimension=0, tiled=True),
    )
    return (
        output,
        input_grad,
        owned_grads[0],
        owned_grads[1],
        owned_grads[2],
        owned_grads[3],
        owned_grads[4],
        owned_grads[5],
        owned_grads[6],
        owned_grads[7],
        owned_grads[8],
        owned_grads[9],
        owned_grads[10],
        owned_grads[11],
        owned_grads[12],
    )


def solution(mesh):
    placed = (
        P("dp", "ctx", None),
        P("dp", "ctx"),
        P("dp", "ctx"),
        P(("dp", "ctx")),
        P(("dp", "ctx")),
        P(("dp", "ctx")),
        P(("dp", "ctx")),
        P(("dp", "ctx"), None),
        P(("dp", "ctx")),
        P(("dp", "ctx")),
        P(("dp", "ctx")),
        P(("dp", "ctx"), None),
        P(("dp", "ctx"), None),
        P(("dp", "ctx")),
        P(("dp", "ctx"), None),
        P(("dp", "ctx")),
        P("dp", "ctx", None),
    )
    return jax.shard_map(
        per_device,
        mesh=mesh,
        in_specs=placed,
        out_specs=(
            P("dp", "ctx", None),
            P("dp", "ctx", None),
            P(("dp", "ctx")),
            P(("dp", "ctx")),
            P(("dp", "ctx")),
            P(("dp", "ctx")),
            P(("dp", "ctx"), None),
            P(("dp", "ctx")),
            P(("dp", "ctx")),
            P(("dp", "ctx")),
            P(("dp", "ctx"), None),
            P(("dp", "ctx"), None),
            P(("dp", "ctx")),
            P(("dp", "ctx"), None),
            P(("dp", "ctx")),
        ),
        check_vma=False,
    )
```

profile of v0, /device:TPU:6, one launch (start us, length us, event | category | flops | bytes accessed | tf_op | source)
XLA Modules:
  0.0 981.9 jit_solution(15206138620532109484)
XLA Ops:
  17.0 41.0 %all-reduce.25 = (bf16[768]{0:T(1024)(128)(2,1)S(1)}, bf16[768]{0:T(1024)(128)(2,1)S(1)}, bf16[3072]{0:T(1024)(128)(2,1)S(1)}, bf16[768]{0:T(1024)(128)(2,1)S(1)...) all-reduce(bf16[768]{0:T(1024)(128)(2,1)S(1)} %dynamic-update-slice, ...), channel_id=1, replica_groups=mesh['dp'=4,'ctx'=8] {'dp','ctx'}, use_global_device_ids=true, to_apply=%add.12 | all-reduce | flops 9216 | bytes 36864
  63.6 7.9 all-gather.7.cloned.1.call-done
  71.5 4.0 fusion.68
  95.6 9.0 all_gather.57
  105.7 21.5 %all-gather.13.cloned.1.call-done = bf16[768,768]{1,0:T(8,128)(2,1)} async-done(((bf16[24,768]{1,0:T(8,128)(2,1)}), bf16[768,768]{1,0:T(8,128)(2,1)}) %all-gather.13.cloned.1.call-update) | async-done | bytes 1179664 | tf_op jit(solution)/shard_map/all_gather | solution.py:149
  134.4 58.3 %all-gather.15.cloned.1.call-done = bf16[768,3072]{1,0:T(8,128)(2,1)} async-done(((bf16[24,3072]{1,0:T(8,128)(2,1)}), bf16[768,3072]{1,0:T(8,128)(2,1)}) %all-gather.15.cloned.1.call-update) | async-done | bytes 4718608 | tf_op jit(solution)/shard_map/all_gather | solution.py:150
  192.7 6.8 fusion.69
  199.6 40.4 %all-gather.11.cloned.1.call-done = bf16[2,2048,768]{1,2,0:T(8,128)(2,1)} async-done(((bf16[2,256,768]{1,2,0:T(8,128)(2,1)}), bf16[2,2048,768]{1,2,0:T(8,128)(2,1)}) %all-gather.11.cloned.1.call-update) | async-done | bytes 6291472 | tf_op jit(solution)/shard_map/all_gather | solution.py:201
  240.0 21.8 %fusion.14 = (f32[2,256,12]{1,2,0:T(8,128)S(1)}, f32[2,12,2048,256]{3,2,1,0:T(8,128)}) fusion(pred[2,256,2048]{1,2,0:T(8,128)(4,1)S(1)} %compare_and_fusion.1, bf16[2,2048,12,64]{1,3,2,0:T(8,128)(2,1)} %bitcast.222, bf16[2,256,12,48]{1,3,2,0:T(8,128)(2,1)S(1)} %copy.120, bf16[2,256,12,8]{1,3,2,0:T(8,128)(2,1)S(1)} %copy-done.22, ...), kind=kOutput, calls=%fused_computation.25 | convolution fusion | flops 1650714624 | bytes 58482688 | tf_op jit(solution)/shard_map/bqhd,bkhd->bqhk/dot_general | solution.py:209
  261.8 26.1 %all-gather.9.cloned.1.call-done = bf16[2,2048,768]{2,1,0:T(8,128)(2,1)} async-done(((bf16[2,256,768]{2,1,0:T(8,128)(2,1)}), bf16[2,2048,768]{2,1,0:T(8,128)(2,1)}) %all-gather.9.cloned.1.call-update) | async-done | bytes 6291472 | tf_op jit(solution)/shard_map/all_gather | solution.py:202
  287.8 8.7 copy.74
  296.6 22.7 %fusion.15 = f32[2,256,12]{1,2,0:T(8,128)S(1)} fusion(f32[2,12,2048,256]{3,2,1,0:T(8,128)} %get-tuple-element.533, f32[2,256,12]{1,2,0:T(8,128)S(1)} %broadcast_maximum_fusion, pred[2,256,2048]{1,2,0:T(8,128)(4,1)S(1)} %compare_and_fusion.1), kind=kLoop, calls=%fused_computation.26 | loop fusion | flops 62908416 | bytes 51429376 | tf_op jit(solution)/shard_map/reduce_sum | solution.py:215
  319.3 31.5 %multiply_reduce_fusion = (f32[2,256,12]{1,2,0:T(8,128)S(1)}, bf16[2,256,12,64]{1,3,2,0:T(8,128)(2,1)S(1)}) fusion(bf16[2,256,12,64]{1,0,3,2:T(2,128)(2,1)S(1)} %copy-done.16, f32[2,256,12]{1,2,0:T(8,128)S(1)} %fusion.15, bf16[2,2048,12,64]{1,3,2,0:T(8,128)(2,1)S(1)} %bitcast.223, f32[2,12,2048,256]{3,2,1,0:T(8,128)} %get-tuple-element.533, ...), kind=kOutput, calls=%fused_computation.91 | convolution fusion | flops 1675487232 | bytes 59318272 | tf_op jit(solution)/shard_map/bqhk,bkhd->bqhd/dot_general | solution.py:216
  355.1 19.4 %convert_reduce_fusion = (f32[3072]{0:T(1024)S(1)}, bf16[512,3072]{1,0:T(8,128)(2,1)}, f32[512,3072]{1,0:T(8,128)S(1)}) fusion(f32[512,3072]{1,0:T(8,128)} %fusion.69, f32[3072]{0:T(1024)S(1)} %convert_element_type.199, bf16[512,768]{1,0:T(8,128)(2,1)S(1)} %bitcast.220, bf16[3072,768]{1,0:T(8,128)(2,1)} %all-gather.17.cloned.1.call-done), kind=kOutput, calls=%fused_computation.32 | convolution fusion | flops 2533880832 | bytes 21258240 | tf_op jit(solution)/shard_map/dot_general | solution.py:60
  374.5 4.3 multiply_convert_fusion
  380.5 5.2 fusion.74
  390.8 7.1 fusion.73
  398.7 418.6 %while.26 = (s32[]{:T(128)}, bf16[2,256,768]{1,2,0:T(8,128)(2,1)}, bf16[2,256,768]{1,2,0:T(8,128)(2,1)}, s32[2,256]{1,0:T(2,128)S(1)}, f32[2,256,768]{1,2,0:T(8,...) while((s32[]{:T(128)}, bf16[2,256,768]{1,2,0:T(8,128)(2,1)}, ...), condition=%wide.region_8.9_spmd.clone, body=%wide.region_7.8_spmd.clone.sunk | while | flops 1030554112 | bytes 84767320 | solution.py:292
  424.2 7.1 collective-permute-done.4
  433.7 14.4 %collective-permute-done.2 = s32[2,256]{1,0:T(2,128)S(1)} collective-permute-done((s32[2,256]{1,0:T(2,128)S(1)}, s32[2,256]{1,0:T(2,128)S(1)}, u32[]{:S(2)}, u32[]{:S(2)}) %collective-permute-start.2) | collective-permute-done | bytes 2080 | tf_op jit(solution)/shard_map/while/body/eval_jaxpr/ppermute | solution.py:19
  473.4 6.0 collective-permute-done.4
  481.8 14.4 %collective-permute-done.2 = s32[2,256]{1,0:T(2,128)S(1)} collective-permute-done((s32[2,256]{1,0:T(2,128)S(1)}, s32[2,256]{1,0:T(2,128)S(1)}, u32[]{:S(2)}, u32[]{:S(2)}) %collective-permute-start.2) | collective-permute-done | bytes 2080 | tf_op jit(solution)/shard_map/while/body/eval_jaxpr/ppermute | solution.py:19
  500.9 3.5 fusion.134
  521.2 6.0 collective-permute-done.4
  529.7 22.9 %collective-permute-done.2 = s32[2,256]{1,0:T(2,128)S(1)} collective-permute-done((s32[2,256]{1,0:T(2,128)S(1)}, s32[2,256]{1,0:T(2,128)S(1)}, u32[]{:S(2)}, u32[]{:S(2)}) %collective-permute-start.2) | collective-permute-done | bytes 2080 | tf_op jit(solution)/shard_map/while/body/eval_jaxpr/ppermute | solution.py:19
  572.7 5.0 collective-permute-done.3
  580.1 10.2 %collective-permute-done.4 = bf16[2,256,768]{1,2,0:T(8,128)(2,1)} collective-permute-done((bf16[2,256,768]{1,2,0:T(8,128)(2,1)}, bf16[2,256,768]{1,2,0:T(8,128)(2,1)}, u32[]{:S(2)}, u32[]{:S(2)}) %collective-permute-start.4) | collective-permute-done | bytes 786464 | tf_op jit(solution)/shard_map/while/body/eval_jaxpr/ppermute | solution.py:24
  592.8 14.4 %collective-permute-done.2 = s32[2,256]{1,0:T(2,128)S(1)} collective-permute-done((s32[2,256]{1,0:T(2,128)S(1)}, s32[2,256]{1,0:T(2,128)S(1)}, u32[]{:S(2)}, u32[]{:S(2)}) %collective-permute-start.2) | collective-permute-done | bytes 2080 | tf_op jit(solution)/shard_map/while/body/eval_jaxpr/ppermute | solution.py:19
  627.2 4.4 collective-permute-done.3
  634.0 6.0 collective-permute-done.4
  642.5 14.4 %collective-permute-done.2 = s32[2,256]{1,0:T(2,128)S(1)} collective-permute-done((s32[2,256]{1,0:T(2,128)S(1)}, s32[2,256]{1,0:T(2,128)S(1)}, u32[]{:S(2)}, u32[]{:S(2)}) %collective-permute-start.2) | collective-permute-done | bytes 2080 | tf_op jit(solution)/shard_map/while/body/eval_jaxpr/ppermute | solution.py:19
  661.5 3.5 fusion.134
  681.7 6.0 collective-permute-done.4
  690.2 22.7 %collective-permute-done.2 = s32[2,256]{1,0:T(2,128)S(1)} collective-permute-done((s32[2,256]{1,0:T(2,128)S(1)}, s32[2,256]{1,0:T(2,128)S(1)}, u32[]{:S(2)}, u32[]{:S(2)}) %collective-permute-start.2) | collective-permute-done | bytes 2080 | tf_op jit(solution)/shard_map/while/body/eval_jaxpr/ppermute | solution.py:19
  717.5 3.5 fusion.134
  733.0 8.6 collective-permute-done.3
  744.0 6.0 collective-permute-done.4
  752.4 14.4 %collective-permute-done.2 = s32[2,256]{1,0:T(2,128)S(1)} collective-permute-done((s32[2,256]{1,0:T(2,128)S(1)}, s32[2,256]{1,0:T(2,128)S(1)}, u32[]{:S(2)}, u32[]{:S(2)}) %collective-permute-start.2) | collective-permute-done | bytes 2080 | tf_op jit(solution)/shard_map/while/body/eval_jaxpr/ppermute | solution.py:19
  786.9 4.9 collective-permute-done.3
  794.2 6.0 collective-permute-done.4
  802.6 14.4 %collective-permute-done.2 = s32[2,256]{1,0:T(2,128)S(1)} collective-permute-done((s32[2,256]{1,0:T(2,128)S(1)}, s32[2,256]{1,0:T(2,128)S(1)}, u32[]{:S(2)}, u32[]{:S(2)}) %collective-permute-start.2) | collective-permute-done | bytes 2080 | tf_op jit(solution)/shard_map/while/body/eval_jaxpr/ppermute | solution.py:19
  822.8 6.6 fusion.51
  830.7 7.2 fusion.71
  838.0 6.2 fusion.70
  844.5 6.1 fusion.63
  853.2 42.0 %all-reduce.24 = (f32[768]{0:T(1024)S(1)}, f32[768]{0:T(1024)S(1)}, f32[768]{0:T(1024)S(1)}, f32[768]{0:T(1024)S(1)}, f32[768]{0:T(1024)S(1)}, /*index=5*/f32[76...) all-reduce(f32[768]{0:T(1024)S(1)} %get-tuple-element.447, ...), channel_id=2, replica_groups=mesh['dp'=4,'ctx'=8] {'dp','ctx'}, use_global_device_ids=true, to_apply=%region_12.13.clone | all-reduce | flops 9216 | bytes 73728
  900.5 3.7 fusion.48
  906.2 68.4 %reduce-scatter.5.cloned.1.call-done = f32[24,2304]{1,0:T(8,128)} async-done(((f32[768,2304]{1,0:T(8,128)}), f32[24,2304]{1,0:T(8,128)}) %reduce-scatter.5.cloned.1.call-update) | async-done | bytes 221200 | tf_op jit(solution)/shard_map/reduce_scatter | solution.py:323
  (444 shorter events, 270.2 us)
Async XLA Ops:
  7.2 64.3 %all-gather.7.cloned.1.call-start = ((), (), s32[]{:S(2)}) async-start(), calls=%async_computation.4 | async-start | bytes 3649536 | tf_op jit(solution)/shard_map/all_gather | solution.py:145
  7.9 119.3 %all-gather.13.cloned.1.call-start = ((), (), s32[]{:S(2)}) async-start(), calls=%async_computation.7 | async-start | bytes 1216512 | tf_op jit(solution)/shard_map/all_gather | solution.py:149
  8.7 184.1 %all-gather.15.cloned.1.call-start = ((), (), s32[]{:S(2)}) async-start(), calls=%async_computation.8 | async-start | bytes 4866048 | tf_op jit(solution)/shard_map/all_gather | solution.py:150
  9.4 230.6 %all-gather.11.cloned.1.call-start = ((), (), s32[]{:S(2)}) async-start(), calls=%async_computation.6 | async-start | bytes 7077888 | tf_op jit(solution)/shard_map/all_gather | solution.py:201
  94.0 193.8 %all-gather.9.cloned.1.call-start = ((), (), s32[]{:S(2)}) async-start(), calls=%async_computation.5 | async-start | bytes 7077888 | tf_op jit(solution)/shard_map/all_gather | solution.py:202
  94.6 260.4 %all-gather.17.cloned.1.call-start = ((), (), s32[]{:S(2)}) async-start(), calls=%async_computation.9 | async-start | bytes 4866048 | tf_op jit(solution)/shard_map/all_gather | solution.py:152
  95.2 811.0 %reduce-scatter.7.cloned.1.call-start = ((), (), s32[]{:S(2)}) async-start(), calls=%async_computation.11 | async-start | bytes 2433024 | tf_op jit(solution)/shard_map/reduce_scatter | solution.py:327
  355.0 551.2 %reduce-scatter.11.cloned.1.call-start = ((), (), s32[]{:S(2)}) async-start(), calls=%async_computation.13 | async-start | bytes 9732096 | tf_op jit(solution)/shard_map/reduce_scatter | solution.py:330
  385.7 520.5 %reduce-scatter.9.cloned.1.call-start = ((), (), s32[]{:S(2)}) async-start(), calls=%async_computation.12 | async-start | bytes 9732096 | tf_op jit(solution)/shard_map/reduce_scatter | solution.py:328
  397.9 576.7 %reduce-scatter.5.cloned.1.call-start = ((), (), s32[]{:S(2)}) async-start(), calls=%async_computation.10 | async-start | bytes 7299072 | tf_op jit(solution)/shard_map/reduce_scatter | solution.py:323
  409.3 12.5 %collective-permute-start.3 = (bf16[2,256,768]{1,2,0:T(8,128)(2,1)}, bf16[2,256,768]{1,2,0:T(8,128)(2,1)}, u32[]{:S(2)}, u32[]{:S(2)}) collective-permute-start(bf16[2,256,768]{1,2,0:T(8,128)(2,1)} %fusion.135), channel_id=1, source_target_pairs={{0,1},{1,2},{2,3},{3,4},{4,5},{5,6},{6,7},{7,0},{8,9},{9,10},{10,1... | collective-permute-start | bytes 2359304 | tf_op jit(solution)/shard_map/while/body/eval_jaxpr/ppermute | solution.py:24
  412.5 18.8 %collective-permute-start.4 = (bf16[2,256,768]{1,2,0:T(8,128)(2,1)}, bf16[2,256,768]{1,2,0:T(8,128)(2,1)}, u32[]{:S(2)}, u32[]{:S(2)}) collective-permute-start(bf16[2,256,768]{1,2,0:T(8,128)(2,1)} %fusion.137), channel_id=1, source_target_pairs={{0,1},{1,2},{2,3},{3,4},{4,5},{5,6},{6,7},{7,0},{8,9},{9,10},{10,1... | collective-permute-start | bytes 2359304 | tf_op jit(solution)/shard_map/while/body/eval_jaxpr/ppermute | solution.py:24
  414.0 34.1 %collective-permute-start = (bf16[2,256,768]{1,2,0:T(8,128)(2,1)S(1)}, bf16[2,256,768]{1,2,0:T(8,128)(2,1)}, u32[]{:S(2)}, u32[]{:S(2)}) collective-permute-start(bf16[2,256,768]{1,2,0:T(8,128)(2,1)S(1)} %copy.138), channel_id=1, source_target_pairs={{0,1},{1,2},{2,3},{3,4},{4,5},{5,6},{6,7},{8,9},{9,10},{10,11},{11... | collective-permute-start | bytes 2359304 | tf_op jit(solution)/shard_map/while/body/eval_jaxpr/ppermute | solution.py:19
  416.1 32.0 %collective-permute-start.1 = (bf16[2,256,768]{1,2,0:T(8,128)(2,1)}, bf16[2,256,768]{1,2,0:T(8,128)(2,1)}, u32[]{:S(2)}, u32[]{:S(2)}) collective-permute-start(bf16[2,256,768]{1,2,0:T(8,128)(2,1)} %copy.139), channel_id=1, source_target_pairs={{0,1},{1,2},{2,3},{3,4},{4,5},{5,6},{6,7},{8,9},{9,10},{10,11},{11... | collective-permute-start | bytes 2359304 | tf_op jit(solution)/shard_map/while/body/eval_jaxpr/ppermute | solution.py:19
  418.1 30.1 %collective-permute-start.2 = (s32[2,256]{1,0:T(2,128)S(1)}, s32[2,256]{1,0:T(2,128)S(1)}, u32[]{:S(2)}, u32[]{:S(2)}) collective-permute-start(s32[2,256]{1,0:T(2,128)S(1)} %copy.140), channel_id=1, source_target_pairs={{0,1},{1,2},{2,3},{3,4},{4,5},{5,6},{6,7},{8,9},{9,10},{10,11},{11... | collective-permute-start | bytes 6152 | tf_op jit(solution)/shard_map/while/body/eval_jaxpr/ppermute | solution.py:19
  458.7 12.3 %collective-permute-start.3 = (bf16[2,256,768]{1,2,0:T(8,128)(2,1)}, bf16[2,256,768]{1,2,0:T(8,128)(2,1)}, u32[]{:S(2)}, u32[]{:S(2)}) collective-permute-start(bf16[2,256,768]{1,2,0:T(8,128)(2,1)} %fusion.135), channel_id=1, source_target_pairs={{0,1},{1,2},{2,3},{3,4},{4,5},{5,6},{6,7},{7,0},{8,9},{9,10},{10,1... | collective-permute-start | bytes 2359304 | tf_op jit(solution)/shard_map/while/body/eval_jaxpr/ppermute | solution.py:24
  461.7 17.7 %collective-permute-start.4 = (bf16[2,256,768]{1,2,0:T(8,128)(2,1)}, bf16[2,256,768]{1,2,0:T(8,128)(2,1)}, u32[]{:S(2)}, u32[]{:S(2)}) collective-permute-start(bf16[2,256,768]{1,2,0:T(8,128)(2,1)} %fusion.137), channel_id=1, source_target_pairs={{0,1},{1,2},{2,3},{3,4},{4,5},{5,6},{6,7},{7,0},{8,9},{9,10},{10,1... | collective-permute-start | bytes 2359304 | tf_op jit(solution)/shard_map/while/body/eval_jaxpr/ppermute | solution.py:24
  461.7 34.6 %collective-permute-start = (bf16[2,256,768]{1,2,0:T(8,128)(2,1)S(1)}, bf16[2,256,768]{1,2,0:T(8,128)(2,1)}, u32[]{:S(2)}, u32[]{:S(2)}) collective-permute-start(bf16[2,256,768]{1,2,0:T(8,128)(2,1)S(1)} %copy.138), channel_id=1, source_target_pairs={{0,1},{1,2},{2,3},{3,4},{4,5},{5,6},{6,7},{8,9},{9,10},{10,11},{11... | collective-permute-start | bytes 2359304 | tf_op jit(solution)/shard_map/while/body/eval_jaxpr/ppermute | solution.py:19
  463.7 32.6 %collective-permute-start.1 = (bf16[2,256,768]{1,2,0:T(8,128)(2,1)}, bf16[2,256,768]{1,2,0:T(8,128)(2,1)}, u32[]{:S(2)}, u32[]{:S(2)}) collective-permute-start(bf16[2,256,768]{1,2,0:T(8,128)(2,1)} %copy.139), channel_id=1, source_target_pairs={{0,1},{1,2},{2,3},{3,4},{4,5},{5,6},{6,7},{8,9},{9,10},{10,11},{11... | collective-permute-start | bytes 2359304 | tf_op jit(solution)/shard_map/while/body/eval_jaxpr/ppermute | solution.py:19
  465.6 30.7 %collective-permute-start.2 = (s32[2,256]{1,0:T(2,128)S(1)}, s32[2,256]{1,0:T(2,128)S(1)}, u32[]{:S(2)}, u32[]{:S(2)}) collective-permute-start(s32[2,256]{1,0:T(2,128)S(1)} %copy.140), channel_id=1, source_target_pairs={{0,1},{1,2},{2,3},{3,4},{4,5},{5,6},{6,7},{8,9},{9,10},{10,11},{11... | collective-permute-start | bytes 6152 | tf_op jit(solution)/shard_map/while/body/eval_jaxpr/ppermute | solution.py:19
  510.0 17.2 %collective-permute-start.4 = (bf16[2,256,768]{1,2,0:T(8,128)(2,1)}, bf16[2,256,768]{1,2,0:T(8,128)(2,1)}, u32[]{:S(2)}, u32[]{:S(2)}) collective-permute-start(bf16[2,256,768]{1,2,0:T(8,128)(2,1)} %fusion.137), channel_id=1, source_target_pairs={{0,1},{1,2},{2,3},{3,4},{4,5},{5,6},{6,7},{7,0},{8,9},{9,10},{10,1... | collective-permute-start | bytes 2359304 | tf_op jit(solution)/shard_map/while/body/eval_jaxpr/ppermute | solution.py:24
  510.0 42.5 %collective-permute-start = (bf16[2,256,768]{1,2,0:T(8,128)(2,1)S(1)}, bf16[2,256,768]{1,2,0:T(8,128)(2,1)}, u32[]{:S(2)}, u32[]{:S(2)}) collective-permute-start(bf16[2,256,768]{1,2,0:T(8,128)(2,1)S(1)} %copy.138), channel_id=1, source_target_pairs={{0,1},{1,2},{2,3},{3,4},{4,5},{5,6},{6,7},{8,9},{9,10},{10,11},{11... | collective-permute-start | bytes 2359304 | tf_op jit(solution)/shard_map/while/body/eval_jaxpr/ppermute | solution.py:19
  512.0 40.5 %collective-permute-start.1 = (bf16[2,256,768]{1,2,0:T(8,128)(2,1)}, bf16[2,256,768]{1,2,0:T(8,128)(2,1)}, u32[]{:S(2)}, u32[]{:S(2)}) collective-permute-start(bf16[2,256,768]{1,2,0:T(8,128)(2,1)} %copy.139), channel_id=1, source_target_pairs={{0,1},{1,2},{2,3},{3,4},{4,5},{5,6},{6,7},{8,9},{9,10},{10,11},{11... | collective-permute-start | bytes 2359304 | tf_op jit(solution)/shard_map/while/body/eval_jaxpr/ppermute | solution.py:19
  513.9 38.6 %collective-permute-start.2 = (s32[2,256]{1,0:T(2,128)S(1)}, s32[2,256]{1,0:T(2,128)S(1)}, u32[]{:S(2)}, u32[]{:S(2)}) collective-permute-start(s32[2,256]{1,0:T(2,128)S(1)} %copy.140), channel_id=1, source_target_pairs={{0,1},{1,2},{2,3},{3,4},{4,5},{5,6},{6,7},{8,9},{9,10},{10,11},{11... | collective-permute-start | bytes 6152 | tf_op jit(solution)/shard_map/while/body/eval_jaxpr/ppermute | solution.py:19
  563.1 14.6 %collective-permute-start.3 = (bf16[2,256,768]{1,2,0:T(8,128)(2,1)}, bf16[2,256,768]{1,2,0:T(8,128)(2,1)}, u32[]{:S(2)}, u32[]{:S(2)}) collective-permute-start(bf16[2,256,768]{1,2,0:T(8,128)(2,1)} %fusion.135), channel_id=1, source_target_pairs={{0,1},{1,2},{2,3},{3,4},{4,5},{5,6},{6,7},{7,0},{8,9},{9,10},{10,1... | collective-permute-start | bytes 2359304 | tf_op jit(solution)/shard_map/while/body/eval_jaxpr/ppermute | solution.py:24
  566.1 24.3 %collective-permute-start.4 = (bf16[2,256,768]{1,2,0:T(8,128)(2,1)}, bf16[2,256,768]{1,2,0:T(8,128)(2,1)}, u32[]{:S(2)}, u32[]{:S(2)}) collective-permute-start(bf16[2,256,768]{1,2,0:T(8,128)(2,1)} %fusion.137), channel_id=1, source_target_pairs={{0,1},{1,2},{2,3},{3,4},{4,5},{5,6},{6,7},{7,0},{8,9},{9,10},{10,1... | collective-permute-start | bytes 2359304 | tf_op jit(solution)/shard_map/while/body/eval_jaxpr/ppermute | solution.py:24
  566.1 41.1 %collective-permute-start = (bf16[2,256,768]{1,2,0:T(8,128)(2,1)S(1)}, bf16[2,256,768]{1,2,0:T(8,128)(2,1)}, u32[]{:S(2)}, u32[]{:S(2)}) collective-permute-start(bf16[2,256,768]{1,2,0:T(8,128)(2,1)S(1)} %copy.138), channel_id=1, source_target_pairs={{0,1},{1,2},{2,3},{3,4},{4,5},{5,6},{6,7},{8,9},{9,10},{10,11},{11... | collective-permute-start | bytes 2359304 | tf_op jit(solution)/shard_map/while/body/eval_jaxpr/ppermute | solution.py:19
  568.1 39.1 %collective-permute-start.1 = (bf16[2,256,768]{1,2,0:T(8,128)(2,1)}, bf16[2,256,768]{1,2,0:T(8,128)(2,1)}, u32[]{:S(2)}, u32[]{:S(2)}) collective-permute-start(bf16[2,256,768]{1,2,0:T(8,128)(2,1)} %copy.139), channel_id=1, source_target_pairs={{0,1},{1,2},{2,3},{3,4},{4,5},{5,6},{6,7},{8,9},{9,10},{10,11},{11... | collective-permute-start | bytes 2359304 | tf_op jit(solution)/shard_map/while/body/eval_jaxpr/ppermute | solution.py:19
  570.0 37.2 %collective-permute-start.2 = (s32[2,256]{1,0:T(2,128)S(1)}, s32[2,256]{1,0:T(2,128)S(1)}, u32[]{:S(2)}, u32[]{:S(2)}) collective-permute-start(s32[2,256]{1,0:T(2,128)S(1)} %copy.140), channel_id=1, source_target_pairs={{0,1},{1,2},{2,3},{3,4},{4,5},{5,6},{6,7},{8,9},{9,10},{10,11},{11... | collective-permute-start | bytes 6152 | tf_op jit(solution)/shard_map/while/body/eval_jaxpr/ppermute | solution.py:19
  617.8 13.8 %collective-permute-start.3 = (bf16[2,256,768]{1,2,0:T(8,128)(2,1)}, bf16[2,256,768]{1,2,0:T(8,128)(2,1)}, u32[]{:S(2)}, u32[]{:S(2)}) collective-permute-start(bf16[2,256,768]{1,2,0:T(8,128)(2,1)} %fusion.135), channel_id=1, source_target_pairs={{0,1},{1,2},{2,3},{3,4},{4,5},{5,6},{6,7},{7,0},{8,9},{9,10},{10,1... | collective-permute-start | bytes 2359304 | tf_op jit(solution)/shard_map/while/body/eval_jaxpr/ppermute | solution.py:24
  620.7 19.3 %collective-permute-start.4 = (bf16[2,256,768]{1,2,0:T(8,128)(2,1)}, bf16[2,256,768]{1,2,0:T(8,128)(2,1)}, u32[]{:S(2)}, u32[]{:S(2)}) collective-permute-start(bf16[2,256,768]{1,2,0:T(8,128)(2,1)} %fusion.137), channel_id=1, source_target_pairs={{0,1},{1,2},{2,3},{3,4},{4,5},{5,6},{6,7},{7,0},{8,9},{9,10},{10,1... | collective-permute-start | bytes 2359304 | tf_op jit(solution)/shard_map/while/body/eval_jaxpr/ppermute | solution.py:24
  620.7 36.2 %collective-permute-start = (bf16[2,256,768]{1,2,0:T(8,128)(2,1)S(1)}, bf16[2,256,768]{1,2,0:T(8,128)(2,1)}, u32[]{:S(2)}, u32[]{:S(2)}) collective-permute-start(bf16[2,256,768]{1,2,0:T(8,128)(2,1)S(1)} %copy.138), channel_id=1, source_target_pairs={{0,1},{1,2},{2,3},{3,4},{4,5},{5,6},{6,7},{8,9},{9,10},{10,11},{11... | collective-permute-start | bytes 2359304 | tf_op jit(solution)/shard_map/while/body/eval_jaxpr/ppermute | solution.py:19
  622.6 34.3 %collective-permute-start.1 = (bf16[2,256,768]{1,2,0:T(8,128)(2,1)}, bf16[2,256,768]{1,2,0:T(8,128)(2,1)}, u32[]{:S(2)}, u32[]{:S(2)}) collective-permute-start(bf16[2,256,768]{1,2,0:T(8,128)(2,1)} %copy.139), channel_id=1, source_target_pairs={{0,1},{1,2},{2,3},{3,4},{4,5},{5,6},{6,7},{8,9},{9,10},{10,11},{11... | collective-permute-start | bytes 2359304 | tf_op jit(solution)/shard_map/while/body/eval_jaxpr/ppermute | solution.py:19
  624.6 32.3 %collective-permute-start.2 = (s32[2,256]{1,0:T(2,128)S(1)}, s32[2,256]{1,0:T(2,128)S(1)}, u32[]{:S(2)}, u32[]{:S(2)}) collective-permute-start(s32[2,256]{1,0:T(2,128)S(1)} %copy.140), channel_id=1, source_target_pairs={{0,1},{1,2},{2,3},{3,4},{4,5},{5,6},{6,7},{8,9},{9,10},{10,11},{11... | collective-permute-start | bytes 6152 | tf_op jit(solution)/shard_map/while/body/eval_jaxpr/ppermute | solution.py:19
  670.5 17.2 %collective-permute-start.4 = (bf16[2,256,768]{1,2,0:T(8,128)(2,1)}, bf16[2,256,768]{1,2,0:T(8,128)(2,1)}, u32[]{:S(2)}, u32[]{:S(2)}) collective-permute-start(bf16[2,256,768]{1,2,0:T(8,128)(2,1)} %fusion.137), channel_id=1, source_target_pairs={{0,1},{1,2},{2,3},{3,4},{4,5},{5,6},{6,7},{7,0},{8,9},{9,10},{10,1... | collective-permute-start | bytes 2359304 | tf_op jit(solution)/shard_map/while/body/eval_jaxpr/ppermute | solution.py:24
  670.5 42.4 %collective-permute-start = (bf16[2,256,768]{1,2,0:T(8,128)(2,1)S(1)}, bf16[2,256,768]{1,2,0:T(8,128)(2,1)}, u32[]{:S(2)}, u32[]{:S(2)}) collective-permute-start(bf16[2,256,768]{1,2,0:T(8,128)(2,1)S(1)} %copy.138), channel_id=1, source_target_pairs={{0,1},{1,2},{2,3},{3,4},{4,5},{5,6},{6,7},{8,9},{9,10},{10,11},{11... | collective-permute-start | bytes 2359304 | tf_op jit(solution)/shard_map/while/body/eval_jaxpr/ppermute | solution.py:19
  672.4 40.5 %collective-permute-start.1 = (bf16[2,256,768]{1,2,0:T(8,128)(2,1)}, bf16[2,256,768]{1,2,0:T(8,128)(2,1)}, u32[]{:S(2)}, u32[]{:S(2)}) collective-permute-start(bf16[2,256,768]{1,2,0:T(8,128)(2,1)} %copy.139), channel_id=1, source_target_pairs={{0,1},{1,2},{2,3},{3,4},{4,5},{5,6},{6,7},{8,9},{9,10},{10,11},{11... | collective-permute-start | bytes 2359304 | tf_op jit(solution)/shard_map/while/body/eval_jaxpr/ppermute | solution.py:19
  674.4 38.6 %collective-permute-start.2 = (s32[2,256]{1,0:T(2,128)S(1)}, s32[2,256]{1,0:T(2,128)S(1)}, u32[]{:S(2)}, u32[]{:S(2)}) collective-permute-start(s32[2,256]{1,0:T(2,128)S(1)} %copy.140), channel_id=1, source_target_pairs={{0,1},{1,2},{2,3},{3,4},{4,5},{5,6},{6,7},{8,9},{9,10},{10,11},{11... | collective-permute-start | bytes 6152 | tf_op jit(solution)/shard_map/while/body/eval_jaxpr/ppermute | solution.py:19
  723.6 18.0 %collective-permute-start.3 = (bf16[2,256,768]{1,2,0:T(8,128)(2,1)}, bf16[2,256,768]{1,2,0:T(8,128)(2,1)}, u32[]{:S(2)}, u32[]{:S(2)}) collective-permute-start(bf16[2,256,768]{1,2,0:T(8,128)(2,1)} %fusion.135), channel_id=1, source_target_pairs={{0,1},{1,2},{2,3},{3,4},{4,5},{5,6},{6,7},{7,0},{8,9},{9,10},{10,1... | collective-permute-start | bytes 2359304 | tf_op jit(solution)/shard_map/while/body/eval_jaxpr/ppermute | solution.py:24
  726.5 23.5 %collective-permute-start.4 = (bf16[2,256,768]{1,2,0:T(8,128)(2,1)}, bf16[2,256,768]{1,2,0:T(8,128)(2,1)}, u32[]{:S(2)}, u32[]{:S(2)}) collective-permute-start(bf16[2,256,768]{1,2,0:T(8,128)(2,1)} %fusion.137), channel_id=1, source_target_pairs={{0,1},{1,2},{2,3},{3,4},{4,5},{5,6},{6,7},{7,0},{8,9},{9,10},{10,1... | collective-permute-start | bytes 2359304 | tf_op jit(solution)/shard_map/while/body/eval_jaxpr/ppermute | solution.py:24
  726.5 40.3 %collective-permute-start = (bf16[2,256,768]{1,2,0:T(8,128)(2,1)S(1)}, bf16[2,256,768]{1,2,0:T(8,128)(2,1)}, u32[]{:S(2)}, u32[]{:S(2)}) collective-permute-start(bf16[2,256,768]{1,2,0:T(8,128)(2,1)S(1)} %copy.138), channel_id=1, source_target_pairs={{0,1},{1,2},{2,3},{3,4},{4,5},{5,6},{6,7},{8,9},{9,10},{10,11},{11... | collective-permute-start | bytes 2359304 | tf_op jit(solution)/shard_map/while/body/eval_jaxpr/ppermute | solution.py:19
  728.4 38.4 %collective-permute-start.1 = (bf16[2,256,768]{1,2,0:T(8,128)(2,1)}, bf16[2,256,768]{1,2,0:T(8,128)(2,1)}, u32[]{:S(2)}, u32[]{:S(2)}) collective-permute-start(bf16[2,256,768]{1,2,0:T(8,128)(2,1)} %copy.139), channel_id=1, source_target_pairs={{0,1},{1,2},{2,3},{3,4},{4,5},{5,6},{6,7},{8,9},{9,10},{10,11},{11... | collective-permute-start | bytes 2359304 | tf_op jit(solution)/shard_map/while/body/eval_jaxpr/ppermute | solution.py:19
  730.4 36.5 %collective-permute-start.2 = (s32[2,256]{1,0:T(2,128)S(1)}, s32[2,256]{1,0:T(2,128)S(1)}, u32[]{:S(2)}, u32[]{:S(2)}) collective-permute-start(s32[2,256]{1,0:T(2,128)S(1)} %copy.140), channel_id=1, source_target_pairs={{0,1},{1,2},{2,3},{3,4},{4,5},{5,6},{6,7},{8,9},{9,10},{10,11},{11... | collective-permute-start | bytes 6152 | tf_op jit(solution)/shard_map/while/body/eval_jaxpr/ppermute | solution.py:19
  777.4 14.4 %collective-permute-start.3 = (bf16[2,256,768]{1,2,0:T(8,128)(2,1)}, bf16[2,256,768]{1,2,0:T(8,128)(2,1)}, u32[]{:S(2)}, u32[]{:S(2)}) collective-permute-start(bf16[2,256,768]{1,2,0:T(8,128)(2,1)} %fusion.135), channel_id=1, source_target_pairs={{0,1},{1,2},{2,3},{3,4},{4,5},{5,6},{6,7},{7,0},{8,9},{9,10},{10,1... | collective-permute-start | bytes 2359304 | tf_op jit(solution)/shard_map/while/body/eval_jaxpr/ppermute | solution.py:24
  780.4 19.8 %collective-permute-start.4 = (bf16[2,256,768]{1,2,0:T(8,128)(2,1)}, bf16[2,256,768]{1,2,0:T(8,128)(2,1)}, u32[]{:S(2)}, u32[]{:S(2)}) collective-permute-start(bf16[2,256,768]{1,2,0:T(8,128)(2,1)} %fusion.137), channel_id=1, source_target_pairs={{0,1},{1,2},{2,3},{3,4},{4,5},{5,6},{6,7},{7,0},{8,9},{9,10},{10,1... | collective-permute-start | bytes 2359304 | tf_op jit(solution)/shard_map/while/body/eval_jaxpr/ppermute | solution.py:24
  780.4 36.6 %collective-permute-start = (bf16[2,256,768]{1,2,0:T(8,128)(2,1)S(1)}, bf16[2,256,768]{1,2,0:T(8,128)(2,1)}, u32[]{:S(2)}, u32[]{:S(2)}) collective-permute-start(bf16[2,256,768]{1,2,0:T(8,128)(2,1)S(1)} %copy.138), channel_id=1, source_target_pairs={{0,1},{1,2},{2,3},{3,4},{4,5},{5,6},{6,7},{8,9},{9,10},{10,11},{11... | collective-permute-start | bytes 2359304 | tf_op jit(solution)/shard_map/while/body/eval_jaxpr/ppermute | solution.py:19
  782.3 34.7 %collective-permute-start.1 = (bf16[2,256,768]{1,2,0:T(8,128)(2,1)}, bf16[2,256,768]{1,2,0:T(8,128)(2,1)}, u32[]{:S(2)}, u32[]{:S(2)}) collective-permute-start(bf16[2,256,768]{1,2,0:T(8,128)(2,1)} %copy.139), channel_id=1, source_target_pairs={{0,1},{1,2},{2,3},{3,4},{4,5},{5,6},{6,7},{8,9},{9,10},{10,11},{11... | collective-permute-start | bytes 2359304 | tf_op jit(solution)/shard_map/while/body/eval_jaxpr/ppermute | solution.py:19
  784.3 32.8 %collective-permute-start.2 = (s32[2,256]{1,0:T(2,128)S(1)}, s32[2,256]{1,0:T(2,128)S(1)}, u32[]{:S(2)}, u32[]{:S(2)}) collective-permute-start(s32[2,256]{1,0:T(2,128)S(1)} %copy.140), channel_id=1, source_target_pairs={{0,1},{1,2},{2,3},{3,4},{4,5},{5,6},{6,7},{8,9},{9,10},{10,11},{11... | collective-permute-start | bytes 6152 | tf_op jit(solution)/shard_map/while/body/eval_jaxpr/ppermute | solution.py:19
  (70 other events, 849.9 us)
Sparse Core Ops, SparseCore 0:
  10.9 60.5 all-gather.6
  74.4 52.7 all-gather.12
  130.1 62.5 all-gather.14
  194.5 45.4 all-gather.10
  242.3 45.5 all-gather.8
  290.6 63.6 all-gather.16
  360.1 116.1 reduce-scatter.6
  483.7 156.9 reduce-scatter.10
  647.3 202.0 reduce-scatter.8
  856.4 118.2 reduce-scatter.4
where the time goes:
time: 996 us; the launch traced here: 982 us
  waiting for transfers between devices  443 us (44%)
  matrix products  195 us (20%)
  other arithmetic  102 us (10%)
  blocking collectives  92 us (9%)
  local copies, waits for them, and re-layouts  84.7 us (9%)
  starting transfers between devices  48.7 us (5%)
  between operations  15.4 us (2%)
    ppermute x24, waiting for transfers between devices, from_behind(): return lax.ppermute(value, axis, pairs)  132 us
    ppermute x16, waiting for transfers between devices, shifted(): lax.ppermute(value, axis, [(i, (i + by) % size) for i in range(size)])  84.6 us
    unnamed x2, blocking collectives  83 us
    reduce_scatter x1, waiting for transfers between devices, per_device(): lax.psum_scatter(d_qkv, ('dp', 'ctx'), scatter_dimension=0, tiled=True)  68.4 us
    all_gather x1, waiting for transfers between devices, per_device(): lax.all_gather(shards[9], ('dp', 'ctx'), axis=0, tiled=True)  58.3 us
    ppermute x24, starting transfers between devices, from_behind(): return lax.ppermute(value, axis, pairs)  46.4 us
    all_gather x1, waiting for transfers between devices, per_device(): key_blk = lax.all_gather(key_flat, 'ctx', axis=1, tiled=True)  40.4 us
    dot_general x4, matrix products, contract_last(): lax.dot_general(left_side, right_side, (((1,), (1,)), ((), ())), preferre...  35.8 us
  transfers between devices with their start and end apart: 50, of which 30 were waited for; matrix products, arithmetic and copies ran while one was open for 38% of the time, Pallas kernels for 0%

commit v1 on v0

--- a/solution.py
+++ b/solution.py
@@ -3,7 +3,9 @@
 import jax
 import jax.numpy as jnp
 from jax import lax
-from jax.sharding import PartitionSpec as P
+from jax.experimental import pallas as pl
+from jax.experimental.pallas import tpu as pltpu
+from jax.sharding import Mesh, PartitionSpec as P
 
 HEAD_DIM = 64
 ROT_DIMS = 16
@@ -349,7 +351,395 @@
     )
 
 
-def solution(mesh):
+LANES = 128
+BLK = 256
+BF = jnp.bfloat16
+F32 = jnp.float32
+SWAP = [(0, 1), (1, 0)]
+CTX_AXES = ("y", "x", "core")
+ALL_AXES = ("dp", "y", "x", "core")
+
+
+def dot_nn(a, b):
+    return lax.dot_general(a, b, (((1,), (0,)), ((), ())), preferred_element_type=F32)
+
+
+def dot_nt(a, b):
+    return lax.dot_general(a, b, (((1,), (1,)), ((), ())), preferred_element_type=F32)
+
+
+def dot_tn(a, b):
+    return lax.dot_general(a, b, (((0,), (0,)), ((), ())), preferred_element_type=F32)
+
+
+def whole(shape):
+    return pl.BlockSpec(shape, lambda *ids: (0,) * len(shape))
+
+
+def pre_body(x_ref, vec_ref, w_ref, b_ref, cs_ref, s1_ref, s2_ref, eq_ref, ek_ref,
+             attn_ref, mlp_ref, q_ref, k_ref, v_ref):
+    x = x_ref[...].astype(F32)
+    centre = x - jnp.mean(x, axis=1, keepdims=True)
+    spread = jnp.mean(centre * centre, axis=1, keepdims=True)
+    xhat = centre * lax.rsqrt(spread + EPSILON)
+    attn_in = (xhat * vec_ref[0:1, :] + vec_ref[1:2, :]).astype(BF)
+    attn_ref[...] = attn_in
+    mlp_ref[...] = (xhat * vec_ref[2:3, :] + vec_ref[3:4, :]).astype(BF)
+    packed = dot_nn(attn_in, w_ref[...]) + b_ref[...]
+    heads = w_ref.shape[1] // (3 * LANES)
+    wide = heads * LANES
+    cs, s1, s2 = cs_ref[...], s1_ref[...], s2_ref[...]
+    half = ROT_DIMS // 2
+
+    def turn(u):
+        return u * cs + pltpu.roll(u, LANES - half, 1) * s1 + pltpu.roll(u, half, 1) * s2
+
+    for h in range(heads):
+        cols = slice(h * LANES, (h + 1) * LANES)
+        q = turn(packed[:, h * LANES : (h + 1) * LANES])
+        q_ref[:, cols] = (q.astype(BF).astype(F32) * (1.0 / math.sqrt(HEAD_DIM)) + eq_ref[...]).astype(BF)
+        k = turn(packed[:, wide + h * LANES : wide + (h + 1) * LANES])
+        k_ref[:, cols] = (k + ek_ref[...]).astype(BF)
+        v_ref[:, cols] = packed[:, 2 * wide + h * LANES : 2 * wide + (h + 1) * LANES].astype(BF)
+
+
+def pre_call(x, vecs, w_pad, b_pad, tables):
+    rows, width = x.shape
+    cols = w_pad.shape[1]
+    third = cols // 3
+    row_block = lambda n: pl.BlockSpec((BLK, n), lambda i: (i, 0))
+    return pl.pallas_call(
+        pre_body,
+        grid=(rows // BLK,),
+        in_specs=[row_block(width), whole(vecs.shape), whole(w_pad.shape), whole(b_pad.shape)]
+        + [row_block(LANES)] * 5,
+        out_specs=[row_block(width)] * 2 + [row_block(third)] * 3,
+        out_shape=[jax.ShapeDtypeStruct((rows, width), BF)] * 2
+        + [jax.ShapeDtypeStruct((rows, third), BF)] * 3,
+        compiler_params=pltpu.CompilerParams(vmem_limit_bytes=40 << 20),
+        cost_estimate=pl.CostEstimate(
+            flops=2 * rows * width * cols, bytes_accessed=rows * (width * 6 + cols * 2 + LANES * 20), transcendentals=0
+        ),
+        name="norm_qkv",
+    )(x, vecs, w_pad, b_pad, *tables)
+
+
+def piece(ref, place, j):
+    return ref[pl.ds(pl.multiple_of((place ^ j) * BLK, BLK), BLK), :]
+
+
+def causal(transposed):
+    rows = lax.broadcasted_iota(jnp.int32, (BLK, BLK), 0)
+    cols = lax.broadcasted_iota(jnp.int32, (BLK, BLK), 1)
+    return cols >= rows if transposed else rows >= cols
+
+
+def row_form(column):
+    return jnp.transpose(jnp.broadcast_to(column, (BLK, LANES)))[0:1, :]
+
+
+def attn_body(place_ref, q_ref, k_ref, v_ref, mixed_ref, full_ref, lse_ref):
+    place = place_ref[0]
+    for i in range(q_ref.shape[0] // BLK):
+        q = piece(q_ref, place, i)
+        scores = [dot_nt(q, piece(k_ref, place, j)) for j in range(i + 1)]
+        scores[i] = jnp.where(causal(False), scores[i], NEG_BIG)
+        top = scores[0]
+        for s in scores[1:]:
+            top = jnp.maximum(top, s)
+        top = jnp.max(top, axis=1, keepdims=True)
+        acc = None
+        total = None
+        for j in range(i + 1):
+            p = jnp.exp(scores[j] - top)
+            total = p if total is None else total + p
+            part = dot_nn(p.astype(BF), piece(v_ref, place, j))
+            acc = part if acc is None else acc + part
+        total = jnp.sum(total, axis=1, keepdims=True)
+        mixed = acc / total
+        here = pl.ds(pl.multiple_of((place ^ i) * BLK, BLK), BLK)
+        full_ref[here, :] = mixed
+        mixed_ref[here, :] = mixed.astype(BF)
+        lse_ref[0, i : i + 1, :] = row_form(top + jnp.log(total))
+
+
+def attn_call(place, q, k, v):
+    rows, cols = q.shape
+    heads = cols // LANES
+    col = pl.BlockSpec((rows, LANES), lambda h, p: (0, h))
+    stats = pl.BlockSpec((1, rows // BLK, BLK), lambda h, p: (h, 0, 0))
+    return pl.pallas_call(
+        attn_body,
+        grid_spec=pltpu.PrefetchScalarGridSpec(
+            num_scalar_prefetch=1, grid=(heads,), in_specs=[col] * 3, out_specs=[col, col, stats]
+        ),
+        out_shape=[
+            jax.ShapeDtypeStruct((rows, cols), BF),
+            jax.ShapeDtypeStruct((rows, cols), F32),
+            jax.ShapeDtypeStruct((heads, rows // BLK, BLK), F32),
+        ],
+        compiler_params=pltpu.CompilerParams(vmem_limit_bytes=48 << 20),
+        cost_estimate=pl.CostEstimate(
+            flops=heads * rows * rows * 2 * LANES * 4, bytes_accessed=rows * cols * 12, transcendentals=heads * rows * rows // 2
+        ),
+        name="attention",
+    )(place, q, k, v)
+
+
+def attn_back_body(place_ref, q_ref, k_ref, v_ref, do_ref, full_ref, lse_ref, cs_ref, s1_ref, s2_ref,
+                   dq_ref, dk_ref, dv_ref, dk_acc, dv_acc):
+    place = place_ref[0]
+    blocks = q_ref.shape[0] // BLK
+    half = ROT_DIMS // 2
+    keep = lax.broadcasted_iota(jnp.int32, (BLK, LANES), 1) < HEAD_DIM
+
+    def unturn(g, here):
+        g = jnp.where(keep, g, 0.0)
+        return (
+            g * cs_ref[here, :]
+            - pltpu.roll(g, LANES - half, 1) * s1_ref[here, :]
+            - pltpu.roll(g, half, 1) * s2_ref[here, :]
+        ).astype(BF)
+
+    for i in reversed(range(blocks)):
+        here = pl.ds(pl.multiple_of((place ^ i) * BLK, BLK), BLK)
+        q = q_ref[here, :]
+        do = do_ref[here, :]
+        delta = row_form(jnp.sum(do.astype(F32) * full_ref[here, :], axis=1, keepdims=True))
+        lse = lse_ref[0, i : i + 1, :]
+        dq = None
+        for j in range(i + 1):
+            k = piece(k_ref, place, j)
+            scores = dot_nt(k, q)
+            if j == i:
+                scores = jnp.where(causal(True), scores, NEG_BIG)
+            p = jnp.exp(scores - lse)
+            dp = dot_nt(piece(v_ref, place, j), do)
+            ds = (p * (dp - delta)).astype(BF)
+            dv = dot_nn(p.astype(BF), do)
+            dk = dot_nn(ds, q)
+            if i == blocks - 1:
+                dv_acc[j] = dv
+                dk_acc[j] = dk
+            else:
+                dv_acc[j] += dv
+                dk_acc[j] += dk
+            part = dot_tn(ds, k)
+            dq = part if dq is None else dq + part
+        dq_ref[here, :] = unturn(dq * (1.0 / math.sqrt(HEAD_DIM)), here)
+        dk_ref[here, :] = unturn(dk_acc[i], here)
+        dv_ref[here, :] = dv_acc[i].astype(BF)
+
+
+def attn_back_call(place, q, k, v, do, full, lse, tables):
+    rows, cols = q.shape
+    heads = cols // LANES
+    col = pl.BlockSpec((rows, LANES), lambda h, p: (0, h))
+    one = pl.BlockSpec((rows, LANES), lambda h, p: (0, 0))
+    stats = pl.BlockSpec((1, rows // BLK, BLK), lambda h, p: (h, 0, 0))
+    return pl.pallas_call(
+        attn_back_body,
+        grid_spec=pltpu.PrefetchScalarGridSpec(
+            num_scalar_prefetch=1,
+            grid=(heads,),
+            in_specs=[col] * 5 + [stats] + [one] * 3,
+            out_specs=[col] * 3,
+            scratch_shapes=[pltpu.VMEM((rows // BLK, BLK, LANES), F32)] * 2,
+        ),
+        out_shape=[jax.ShapeDtypeStruct((rows, cols), BF)] * 3,
+        compiler_params=pltpu.CompilerParams(vmem_limit_bytes=48 << 20),
+        cost_estimate=pl.CostEstimate(
+            flops=heads * rows * rows * 5 * LANES * 4, bytes_accessed=rows * cols * 18, transcendentals=heads * rows * rows // 2
+        ),
+        name="attention_back",
+    )(place, q, k, v, do, full, lse, *tables)
+
+
+def swap(value, axis):
+    return lax.ppermute(value, axis, SWAP)
+
+
+def gather_tokens(array, core):
+    own = lax.dynamic_index_in_dim(array, core, 0, keepdims=False)
+    other = lax.dynamic_index_in_dim(array, 1 - core, 0, keepdims=False)
+    own_x, own_y = swap(own, "x"), swap(own, "y")
+    mate = swap(other, "core")
+    mate_y, mate_x = swap(mate, "y"), swap(mate, "x")
+    own_xy = swap(own_x, "y")
+    mate_xy = swap(mate_y, "x")
+    return jnp.concatenate([own, mate, own_x, mate_x, own_y, mate_y, own_xy, mate_xy], axis=0)
+
+
+def scatter_tokens(array, core):
+    part = array.reshape((8, -1) + array.shape[1:])
+    add = lambda a, b: a.astype(F32) + b.astype(F32)
+    low = lambda a: a.astype(BF)
+    mate1, mate3 = swap(part[3], "x"), swap(part[7], "x")
+    own2, own3 = swap(part[4], "y"), swap(part[6], "y")
+    mate_here, mate_far = add(part[1], mate1), low(add(part[5], mate3))
+    own_here, own_far = add(part[0], own2), low(add(part[2], own3))
+    mate_sum = low(add(mate_here, swap(mate_far, "y")))
+    mate_got = swap(mate_sum, "core").astype(F32)
+    own_sum = add(own_here, swap(own_far, "x"))
+    return jnp.stack([jnp.where(core == 0, own_sum, mate_got), jnp.where(core == 0, mate_got, own_sum)])
+
+
+def pick(first, second, core):
+    return jnp.where(core == 0, first, second)
+
+
+def halves_sum(halves, core):
+    first, second = halves
+    got = swap(pick(second, first, core).astype(BF), "core")
+    return (pick(first, second, core) + got.astype(F32)).astype(BF)
+
+
+def split_device(tokens, segments, positions, gain_attn, shift_attn, gain_mlp, shift_mlp, qkv_weight,
+                 query_bias, key_bias, value_bias, dense_weight, expand_weight, expand_bias,
+                 contract_weight, output_bias, cotangent):
+    seqs, toks, width = tokens.shape
+    rows = 8 * toks
+    share = qkv_weight.shape[0]
+    hidden_share = contract_weight.shape[0]
+    n_dp = lax.axis_size("dp")
+    heads = width // HEAD_DIM // 4
+    band = heads * HEAD_DIM
+    core = lax.axis_index("core")
+    chip = lax.axis_index("y") * 2 + lax.axis_index("x")
+    place = chip * 2 + core
+    dp_here = lax.axis_index("dp")
+    hop = [((z * 4 + t), (t * 4 + z)) for z in range(4) for t in range(4)]
+
+    qkv_cols = qkv_weight.reshape(share, 3, 4, band).transpose(2, 0, 1, 3).reshape(4, share, 2, 3 * band // 2)
+    qkv_cols = qkv_cols.transpose(0, 2, 1, 3).reshape(8, share, 3 * band // 2)
+    exp_cols = expand_weight.reshape(share, n_dp, 8, hidden_share).transpose(2, 0, 1, 3)
+    exp_cols = exp_cols.reshape(8, share, n_dp * hidden_share)
+    cols = lax.all_to_all(jnp.concatenate([qkv_cols, exp_cols], axis=2), CTX_AXES, 0, 0, tiled=True)
+    cols = cols.reshape(8 * share, -1)
+    qkv_half = lax.all_gather(cols[:, : 3 * band // 2], "dp", axis=0, tiled=True)
+    qkv_mate = swap(qkv_half, "core")
+    qkv_here = jnp.concatenate([pick(qkv_half, qkv_mate, core), pick(qkv_mate, qkv_half, core)], axis=1)
+    w_pad = jnp.pad(qkv_here.reshape(width, 3 * heads, HEAD_DIM), ((0, 0), (0, 0), (0, LANES - HEAD_DIM)))
+    w_pad = w_pad.reshape(width, 3 * heads * LANES)
+
+    small = jnp.concatenate([gain_attn, shift_attn, gain_mlp, shift_mlp, query_bias, key_bias, value_bias,
+                             output_bias, expand_bias])
+    small = lax.all_gather(small, ALL_AXES, axis=0, tiled=False).astype(F32)
+    vectors = [small[:, n * share : (n + 1) * share].reshape(width) for n in range(8)]
+    vecs = jnp.stack(vectors[:4])
+    out_bias = vectors[7]
+    biases = jnp.stack([lax.dynamic_slice(v, (chip * band,), (band,)) for v in vectors[4:7]])
+    b_pad = jnp.pad(biases.reshape(3 * heads, HEAD_DIM), ((0, 0), (0, LANES - HEAD_DIM))).reshape(1, -1)
+    exp_bias = small[:, 8 * share :].reshape(n_dp, 4, 2, hidden_share)
+    exp_bias = lax.dynamic_index_in_dim(exp_bias, chip, 1, keepdims=False).transpose(1, 0, 2).reshape(1, -1)
+
+    marks = lax.all_gather(jnp.stack([segments, positions]), CTX_AXES, axis=0, tiled=False)
+    marks = lax.dynamic_index_in_dim(marks, core, 2, keepdims=False)
+    marks = jnp.take(marks, place ^ jnp.arange(8), axis=0)
+    seg, pos = marks[:, 0].reshape(rows, 1), marks[:, 1].reshape(rows, 1)
+    lane = jnp.arange(LANES)[None, :]
+    half = ROT_DIMS // 2
+    inverse = jnp.exp((lane % half).astype(F32) * (-2.0 * math.log(10000.0) / ROT_DIMS))
+    angle = pos.astype(F32) * inverse
+    cosine, sine = jnp.cos(angle), jnp.sin(angle)
+    table_c = jnp.where(lane < ROT_DIMS, cosine, jnp.where(lane < HEAD_DIM, 1.0, 0.0))
+    table_1 = jnp.where(lane < half, -sine, 0.0)
+    table_2 = jnp.where((lane >= half) & (lane < ROT_DIMS), sine, 0.0)
+    docs = 16
+    in_doc = (lane >= HEAD_DIM) & (lane < HEAD_DIM + docs)
+    same = in_doc & (lane - HEAD_DIM == seg)
+    mark_q = jnp.where(same, 1.0, 0.0)
+    mark_k = jnp.where(in_doc & ~same, NEG_BIG, 0.0)
+
+    x_rows = gather_tokens(tokens, core)
+    exp_half = lax.all_gather(cols[:, 3 * band // 2 :], "dp", axis=0, tiled=True)
+    dense_moved = lax.ppermute(dense_weight, ("dp", "y", "x"), hop)
+    low_rows = lax.all_gather(jnp.concatenate([contract_weight, dense_moved], axis=0), "dp", axis=0, tiled=False)
+    dy_rows = gather_tokens(cotangent, core)
+
+    attn_in, mlp_in, q, k, v = pre_call(x_rows, vecs, w_pad, b_pad, (table_c, table_1, table_2, mark_q, mark_k))
+    place_arr = place.reshape(1).astype(jnp.int32)
+    mixed, mixed_full, lse = attn_call(place_arr, q, k, v)
+
+    exp_mate = swap(exp_half, "core")
+    w_exp = jnp.concatenate([pick(exp_half, exp_mate, core), pick(exp_mate, exp_half, core)], axis=1)
+    low_mate = swap(low_rows, "core")
+    low_both = jnp.stack([pick(low_rows, low_mate, core), pick(low_mate, low_rows, core)])
+    w_con = low_both[:, :, :hidden_share].reshape(2 * n_dp * hidden_share, width)
+    w_den = low_both[:, :, hidden_share:].transpose(1, 0, 2, 3).reshape(heads, HEAD_DIM, width)
+    w_den = jnp.pad(w_den, ((0, 0), (0, LANES - HEAD_DIM), (0, 0))).reshape(heads * LANES, width)
+
+    hidden_pre = dot_nn(mlp_in, w_exp) + exp_bias
+    hidden = exact_gelu(hidden_pre).astype(BF)
+    out_part = (dot_nn(mixed, w_den) + dot_nn(hidden, w_con)).astype(BF)
+    out_sum = scatter_tokens(out_part, core)
+    output = (tokens.astype(F32) + out_sum + out_bias).astype(BF)
+
+    d_hidden = dot_nt(dy_rows, w_con)
+    _, gelu_pull = jax.vjp(exact_gelu, hidden_pre)
+    d_hidden_pre = gelu_pull(d_hidden)[0].astype(BF)
+    d_mixed = dot_nt(dy_rows, w_den).astype(BF)
+    d_con = dot_tn(hidden, dy_rows)
+    d_exp = dot_tn(mlp_in, d_hidden_pre)
+    d_den = dot_tn(mixed, dy_rows)
+    half_rows = n_dp * hidden_share
+    con_sum = halves_sum((d_con[:half_rows], d_con[half_rows:]), core).reshape(n_dp, hidden_share, width)
+    d_den = d_den.reshape(heads, LANES, width)[:, :HEAD_DIM].reshape(4, 2, share, width)
+    den_sum = halves_sum((d_den[:, 0], d_den[:, 1]), core)
+    exp_sum = halves_sum((d_exp[:, :half_rows], d_exp[:, half_rows:]), core)
+    low_sum = lax.psum_scatter(jnp.concatenate([con_sum, den_sum], axis=1), "dp", scatter_dimension=0, tiled=False)
+    grad_contract = low_sum[:hidden_share].astype(F32)
+    grad_dense = lax.ppermute(low_sum[hidden_share:], ("dp", "y", "x"), hop).astype(F32)
+    exp_own = lax.psum_scatter(exp_sum, "dp", scatter_dimension=0, tiled=True)
+    exp_own = lax.all_to_all(exp_own.reshape(8, share, half_rows), CTX_AXES, 0, 0, tiled=True)
+    grad_expand = exp_own.reshape(8, share, n_dp, hidden_share).transpose(1, 2, 0, 3).reshape(share, -1).astype(F32)
+
+    dq, dk, dv = attn_back_call(place_arr, q, k, v, d_mixed, mixed_full, lse, (table_c, table_1, table_2))
+    d_packed = jnp.concatenate([dq, dk, dv], axis=1)
+    e_attn = dot_nt(d_packed, w_pad)
+    e_mlp = dot_nt(d_hidden_pre, w_exp)
+    xf = x_rows.astype(F32)
+    centre = xf - jnp.mean(xf, axis=1, keepdims=True)
+    xhat = centre * lax.rsqrt(jnp.mean(centre * centre, axis=1, keepdims=True) + EPSILON)
+    d_gain_attn = jnp.sum(e_attn * xhat, axis=0)
+    d_shift_attn = jnp.sum(e_attn, axis=0)
+    d_gain_mlp = jnp.sum(e_mlp * xhat, axis=0)
+    d_shift_mlp = jnp.sum(e_mlp, axis=0)
+    pull = (e_attn * vecs[0] + e_mlp * vecs[2]).astype(BF)
+    ge = scatter_tokens(pull, core)
+    own = tokens.astype(F32)
+    own_c = own - jnp.mean(own, axis=2, keepdims=True)
+    own_r = lax.rsqrt(jnp.mean(own_c * own_c, axis=2, keepdims=True) + EPSILON)
+    own_h = own_c * own_r
+    back = own_r * (ge - jnp.mean(ge, axis=2, keepdims=True) - own_h * jnp.mean(ge * own_h, axis=2, keepdims=True))
+    input_grad = (cotangent.astype(F32) + back).astype(BF)
+
+    d_qkv = dot_tn(attn_in, d_packed).reshape(width, 3 * heads, LANES)[:, :, :HEAD_DIM].reshape(width, 3 * band)
+    qkv_sum = halves_sum((d_qkv[:, : 3 * band // 2], d_qkv[:, 3 * band // 2 :]), core)
+    qkv_own = lax.psum_scatter(qkv_sum, "dp", scatter_dimension=0, tiled=True)
+    qkv_own = lax.all_to_all(qkv_own.reshape(8, share, 3 * band // 2), CTX_AXES, 0, 0, tiled=True)
+    grad_qkv = qkv_own.reshape(4, 2, share, 3 * band // 2).transpose(0, 2, 1, 3).reshape(4, share, 3, band)
+    grad_qkv = grad_qkv.transpose(1, 2, 0, 3).reshape(share, -1).astype(F32)
+
+    d_bias = jnp.sum(d_packed.astype(F32), axis=0).reshape(3, heads, LANES)[:, :, :HEAD_DIM].reshape(3, band)
+    d_exp_bias = jnp.sum(d_hidden_pre.astype(F32), axis=0).reshape(2, n_dp, hidden_share).transpose(1, 0, 2)
+    d_out_bias = jnp.sum(cotangent.astype(F32), axis=(0, 1))
+    lines = [v.reshape(-1, share) for v in (d_gain_attn, d_shift_attn, d_gain_mlp, d_shift_mlp)]
+    for n in range(3):
+        line = lax.dynamic_update_slice(jnp.zeros((width,), F32), d_bias[n], (chip * band,))
+        lines.append(line.reshape(-1, share))
+    lines.append(d_out_bias.reshape(-1, share))
+    line = jnp.zeros((n_dp, 4, 2, hidden_share), F32)
+    line = lax.dynamic_update_slice(line, d_exp_bias[:, None], (0, chip, 0, 0))
+    lines.append(line.reshape(-1, hidden_share))
+    small_grads = lax.all_to_all(jnp.concatenate(lines, axis=1), ALL_AXES, 0, 0, tiled=True)
+    small_grads = jnp.sum(small_grads, axis=0)
+    part = [small_grads[n * share : (n + 1) * share] for n in range(8)]
+    return (output, input_grad, part[0], part[1], part[2], part[3], grad_qkv, part[4], part[5], part[6],
+            grad_dense, grad_expand, small_grads[8 * share :], grad_contract, part[7])
+
+
+def general_plan(mesh):
     placed = (
         P("dp", "ctx", None),
         P("dp", "ctx"),
@@ -392,3 +782,24 @@
         ),
         check_vma=False,
     )
+
+
+def split_plan(mesh):
+    fine = Mesh(mesh.devices.reshape(mesh.shape["dp"], 2, 2, 2), ALL_AXES)
+    tok = P("dp", CTX_AXES, None)
+    mark = P("dp", CTX_AXES)
+    vec = P(ALL_AXES)
+    mat = P(ALL_AXES, None)
+    return jax.shard_map(
+        split_device,
+        mesh=fine,
+        in_specs=(tok, mark, mark, vec, vec, vec, vec, mat, vec, vec, vec, mat, mat, vec, mat, vec, tok),
+        out_specs=(tok, tok, vec, vec, vec, vec, mat, vec, vec, vec, mat, mat, vec, mat, vec),
+        check_vma=False,
+    )
+
+
+def solution(mesh):
+    if mesh.shape["ctx"] == 8 and mesh.shape["dp"] == 4:
+        return split_plan(mesh)
+    return general_plan(mesh)

time: 996 us -> 465 us (0.47)
  waiting for transfers between devices: 443 us -> 55.9 us
  matrix products: 195 us -> 66.2 us
  Pallas kernels: 0 us -> 64.4 us
  other arithmetic: 102 us -> 43 us
  local copies, waits for them, and re-layouts: 84.7 us -> 50.9 us
  blocking collectives: 92 us -> 109 us
    ppermute x40 -> x37, waiting for transfers between devices: 217 us -> 52 us  [the longest x35 49.3 us: swap(): return lax.ppermute(value, axis, SWAP)]
    all_gather x6 -> x0, waiting for transfers between devices: 154 us -> none  [the longest x1 58.3 us: per_device(): lax.all_gather(shards[9], ('dp', 'ctx'), axis=0, tiled=True)]
    dot_general x54 -> x11, matrix products: 195 us -> 66.2 us  [the longest x4 33.2 us: dot_nt(): lax.dot_general(a, b, (((1,), (1,)), ((), ())), preferred_element_type=F32)]
    reduce_scatter x4 -> x3, waiting for transfers between devices: 68.4 us -> 0.02 us  [the longest x1 0.01 us: split_device(): qkv_own = lax.psum_scatter(qkv_sum, 'dp', scatter_dimension=0, tiled=True)]
    pallas_call x0 -> x3, Pallas kernels: none -> 64.4 us  [the longest x1 36.5 us: attn_back_call(): pl.pallas_call(attn_back_body, grid_spec=pltpu.PrefetchScalarGridSpec(num...]
    all_gather x1 -> x4, blocking collectives: 8.96 us -> 59.5 us  [the longest x1 18.5 us: split_device(): lax.all_gather(jnp.concatenate([contract_weight, dense_moved], axis=0), '...]
    unnamed x2 -> x1, blocking collectives: 83 us -> 38.4 us
    convert_element_type x45 -> x16, other arithmetic: 65.7 us -> 23.5 us  [the longest x4 7.08 us: halves_sum(): return (pick(first, second, core) + got.astype(F32)).astype(BF)]
  transfers between devices with their start and end apart: 50 -> 43, of which waited for: 30 -> 14; matrix products, arithmetic and copies ran while one was open for 38% -> 22% of each run, Pallas kernels for 0% -> 0%
where the time goes in v1:
time: 465 us; the launch traced here: 458 us
  blocking collectives  109 us (23%)
  matrix products  66.2 us (14%)
  Pallas kernels  64.4 us (14%)
  waiting for transfers between devices  55.9 us (12%)
  starting transfers between devices  53.3 us (11%)
  local copies, waits for them, and re-layouts  50.9 us (11%)
  other arithmetic  43 us (9%)
  between operations  15.6 us (3%)
    ppermute x35, waiting for transfers between devices, swap(): return lax.ppermute(value, axis, SWAP)  49.3 us
    unnamed x1, blocking collectives  38.4 us
    pallas_call x1, Pallas kernels, attn_back_call(): pl.pallas_call(attn_back_body, grid_spec=pltpu.PrefetchScalarGridSpec(num...  36.5 us
    dot_general x4, matrix products, dot_nt(): lax.dot_general(a, b, (((1,), (1,)), ((), ())), preferred_element_type=F32)  33.2 us
    unnamed x150, local copies, waits for them, and re-layouts  27 us
    ppermute x35, starting transfers between devices, swap(): return lax.ppermute(value, axis, SWAP)  25.2 us
    dot_general x4, matrix products, dot_tn(): lax.dot_general(a, b, (((0,), (0,)), ((), ())), preferred_element_type=F32)  19.3 us
    all_gather x1, blocking collectives, split_device(): lax.all_gather(jnp.concatenate([contract_weight, dense_moved], axis=0), '...  18.5 us
  transfers between devices with their start and end apart: 43, of which 14 were waited for; matrix products, arithmetic and copies ran while one was open for 22% of the time, Pallas kernels for 0%

profile of v1, /device:TPU:6, one launch (start us, length us, event | category | flops | bytes accessed | tf_op | source)
XLA Modules:
  0.0 458.1 jit_solution(11813785525480849094)
XLA Ops:
  7.2 2.1 constant_dynamic-update-slice_fusion.15
  10.0 7.8 %collective-permute-start.8 = (bf16[24,768]{1,0:T(8,128)(2,1)}, bf16[24,768]{1,0:T(8,128)(2,1)S(1)}, u32[]{:S(2)}, u32[]{:S(2)}) collective-permute-start(bf16[24,768]{1,0:T(8,128)(2,1)} %param.28), channel_id=1, source_target_pairs={{0,0},{2,8},{4,16},{6,24},{8,2},{10,10},{12,18},{14,26},{16,4},{18... | collective-permute-start | bytes 110600 | tf_op jit(solution)/shard_map/ppermute | solution.py:656
  21.5 4.2 all-to-all-start
  27.9 38.4 %all-reduce.3 = bf16[9216]{0:T(1024)(128)(2,1)S(1)} all-reduce(bf16[9216]{0:T(1024)(128)(2,1)S(1)} %dynamic-update-slice), channel_id=2, replica_groups=mesh['dp'=4,'y'=2,'x'=2,'core'=2] {'dp','y','x','core'}, use_global_device_ids=true, to_apply=%add.3 | all-reduce | flops 9216 | bytes 36864
  68.5 9.0 %all-gather.1 = s32[16,2,256]{2,1,0:T(2,128)S(1)} all-gather(s32[2,2,256]{2,1,0:T(2,128)S(1)} %pad_add_fusion), channel_id=3, replica_groups=mesh['dp'=4,'y'=2,'x'=2,'core'=2] {'y','x','core'}, dimensions={0}, use_global_device_ids=true | all-gather | bytes 36864 | tf_op jit(solution)/shard_map/all_gather | solution.py:636
  80.9 5.7 %fusion.24 = (f32[2048,128]{1,0:T(8,128)S(1)}, f32[2048,128]{1,0:T(8,128)}, f32[2048,128]{1,0:T(8,128)}) fusion(f32[128]{0:T(128)S(1)} %get-tuple-element.107, f32[2048]{0:T(1024)S(1)} %bitcast.170, pred[128]{0:T(512)(128)(4,1)S(1)} %get-tuple-element.104, pred[128]{0:T(512)(128)(4,1)S(1)} %get-tuple-element.105, f32[128]{0:T(128)S(1)} %get-tuple-element.106, ...), kind=kLoop, calls=%fused_computation.51 | loop fusion | flops 1310720 | bytes 3155328 | tf_op jit(solution)/shard_map/jit(_where)/select_n | solution.py:647
  89.3 18.5 %all-gather.2 = bf16[480,768]{1,0:T(8,128)(2,1)} all-gather(bf16[120,768]{1,0:T(8,128)(2,1)S(1)} %pad_maximum_fusion.9), channel_id=4, replica_groups=mesh['dp'=4,'y'=2,'x'=2,'core'=2] {'dp'}, dimensions={0}, use_global_device_ids=true | all-gather | bytes 921600 | tf_op jit(solution)/shard_map/all_gather | solution.py:657
  108.0 15.6 %all_gather.31 = bf16[768,384]{1,0:T(8,128)(2,1)S(1)} all-gather(bf16[192,384]{1,0:T(8,128)(2,1)S(1)} %slice.260), channel_id=1, replica_groups=mesh['dp'=4,'y'=2,'x'=2,'core'=2] {'dp'}, dimensions={0}, use_global_device_ids=true | all-gather | bytes 737280 | tf_op jit(solution)/shard_map/all_gather | solution.py:655
  123.6 16.3 %all_gather.26 = bf16[768,288]{1,0:T(8,128)(2,1)S(1)} all-gather(bf16[192,288]{1,0:T(8,128)(2,1)S(1)} %slice.254), channel_id=1, replica_groups=mesh['dp'=4,'y'=2,'x'=2,'core'=2] {'dp'}, dimensions={0}, use_global_device_ids=true | all-gather | bytes 552960 | tf_op jit(solution)/shard_map/all_gather | solution.py:619
  142.5 1.8 constant_dynamic-update-slice_fusion.13
  145.8 1.8 constant_dynamic-update-slice_fusion.6
  152.9 2.7 copy.138.w_ref
  158.1 8.9 %collective-permute-done.20 = bf16[256,768]{1,0:T(8,128)(2,1)S(1)} collective-permute-done((bf16[256,768]{1,0:T(8,128)(2,1)}, bf16[256,768]{1,0:T(8,128)(2,1)S(1)}, u32[]{:S(2)}, u32[]{:S(2)}) %collective-permute-start.20) | collective-permute-done | bytes 393248 | tf_op jit(solution)/shard_map/ppermute | solution.py:559
  174.4 4.8 %collective-permute-done.4 = bf16[256,768]{1,0:T(8,128)(2,1)S(1)} collective-permute-done((bf16[256,768]{1,0:T(8,128)(2,1)}, bf16[256,768]{1,0:T(8,128)(2,1)S(1)}, u32[]{:S(2)}, u32[]{:S(2)}) %collective-permute-start.4) | collective-permute-done | bytes 393248 | tf_op jit(solution)/shard_map/ppermute | solution.py:559
  180.9 6.8 %collective-permute-done.23 = bf16[256,768]{1,0:T(8,128)(2,1)S(1)} collective-permute-done((bf16[256,768]{1,0:T(8,128)(2,1)}, bf16[256,768]{1,0:T(8,128)(2,1)S(1)}, u32[]{:S(2)}, u32[]{:S(2)}) %collective-permute-start.23) | collective-permute-done | bytes 393248 | tf_op jit(solution)/shard_map/ppermute | solution.py:559
  187.7 6.4 %collective-permute-done.5 = bf16[256,768]{1,0:T(8,128)(2,1)S(1)} collective-permute-done((bf16[256,768]{1,0:T(8,128)(2,1)}, bf16[256,768]{1,0:T(8,128)(2,1)S(1)}, u32[]{:S(2)}, u32[]{:S(2)}) %collective-permute-start.5) | collective-permute-done | bytes 393248 | tf_op jit(solution)/shard_map/ppermute | solution.py:559
  194.9 3.0 convolution_convert_fusion.do_ref
  199.5 10.6 %norm_qkv.1 = (bf16[2048,768]{1,0:T(8,128)(2,1)}, bf16[2048,768]{1,0:T(8,128)(2,1)}, bf16[2048,384]{1,0:T(8,128)(2,1)S(1)}, bf16[2048,384]{1,0:T(8,128)(2,1)S(1)}, bf16[2048,384]{1,0:T(8,128)(2,1)S(1)}) custom-call(bf16[2048,768]{1,0:T(8,128)(2,1)} %copy-done.10, f32[4,768]{1,0:T(4,128)S(1)} %pad_maximum_fusion.10.vec_ref, ...), custom_call_target="tpu_custom_call" | custom-call | flops 3623878656 | bytes 19398656 | tf_op jit(solution)/shard_map/norm_qkv/pallas_call | solution.py:411
  211.3 17.3 %attention.1 = (bf16[2048,384]{1,0:T(8,128)(2,1)S(1)}, f32[2048,384]{1,0:T(8,128)}, f32[3,8,256]{2,1,0:T(8,128)S(1)}) custom-call(s32[1]{0:T(128)} %bitcast.place_ref, bf16[2048,384]{1,0:T(8,128)(2,1)S(1)} %get-tuple-element.26.q_ref, bf16[2048,384]{1,0:T(8,128)(2,1)S(1)} %get-tuple-element.27.k_ref, bf16[2048,384]{1,0:T(8,128)(2,1)} %copy-done.6), custom_call_target="tpu_custom_call" | custom-call | flops 12884901888 | bytes 9437184 | tf_op jit(solution)/shard_map/attention/pallas_call | solution.py:471
  228.6 36.5 %attention_back.1 = (bf16[2048,384]{1,0:T(8,128)(2,1)S(1)}, bf16[2048,384]{1,0:T(8,128)(2,1)}, bf16[2048,384]{1,0:T(8,128)(2,1)}) custom-call(s32[1]{0:T(128)} %bitcast.place_ref, bf16[2048,384]{1,0:T(8,128)(2,1)} %copy-done.4, bf16[2048,384]{1,0:T(8,128)(2,1)} %copy-done.5, bf16[2048,384]{1,0:T(8,128)(2,1)} %copy-done.6, ...), custom_call_target="tpu_custom_call" | custom-call | flops 32212254720 | bytes 14155776 | tf_op jit(solution)/shard_map/attention_back/pallas_call | solution.py:540
  268.0 2.1 copy-done.17
  270.1 6.3 %fusion.57 = f32[2048,768]{1,0:T(8,128)} fusion(bf16[2048,1152]{1,0:T(8,128)(2,1)S(1)} %constant_dynamic-update-slice_fusion.16, bf16[768,1152]{0,1:T(8,128)(2,1)S(1)} %bitcast.143), kind=kOutput, calls=%fused_computation.175 | convolution fusion | flops 3623878656 | bytes 12779520 | tf_op jit(solution)/shard_map/dot_general | solution.py:368
  276.5 2.6 fusion.35
  279.1 18.3 %convert_reduce_fusion.2 = (f32[768]{0:T(1024)}, bf16[2048,768]{1,0:T(8,128)(2,1)}, f32[2048,768]{1,0:T(8,128)S(1)}) fusion(f32[2048,768]{1,0:T(8,128)S(1)} %fusion.35, f32[768]{0:T(1024)S(1)} %add.186, bf16[2048,768]{1,0:T(8,128)(2,1)S(1)} %copy-done.40, bf16[768,768]{1,0:T(8,128)(2,1)S(1)} %bitcast.153), kind=kOutput, calls=%fused_computation.13 | convolution fusion | flops 2533883136 | bytes 20060160 | tf_op jit(solution)/shard_map/dot_general | solution.py:368
  298.5 6.1 %fusion.59 = f32[768,768]{1,0:T(8,128)} fusion(bf16[2048,768]{1,0:T(8,128)(2,1)S(1)} %multiply_convert_fusion, bf16[2048,768]{1,0:T(8,128)(2,1)} %copy-done.39), kind=kOutput, calls=%fused_computation.177 | convolution fusion | flops 2415919104 | bytes 8650752 | tf_op jit(solution)/shard_map/dot_general | solution.py:372
  304.6 4.7 %fusion.56 = f32[2048,768]{1,0:T(8,128)} fusion(bf16[2048,768]{1,0:T(8,128)(2,1)S(1)} %multiply_convert_fusion, bf16[768,768]{1,0:T(8,128)(2,1)S(1)} %bitcast.154), kind=kOutput, calls=%fused_computation.174 | convolution fusion | flops 2415919104 | bytes 10616832 | tf_op jit(solution)/shard_map/dot_general | solution.py:364
  314.8 7.6 %fusion.58 = f32[768,1152]{0,1:T(8,128)S(1)} fusion(bf16[2048,768]{1,0:T(8,128)(2,1)} %get-tuple-element.36, bf16[2048,1152]{1,0:T(8,128)(2,1)} %copy-done.16), kind=kOutput, calls=%fused_computation.176 | convolution fusion | flops 3623878656 | bytes 11403264 | tf_op jit(solution)/shard_map/dot_general | solution.py:372
  325.1 4.2 fusion.61
  329.3 5.6 %fusion.47 = (f32[768]{0:T(1024)S(1)}, f32[768]{0:T(1024)S(1)}, bf16[2048,768]{1,0:T(8,128)(2,1)}, f32[768]{0:T(1024)S(1)}, f32[768]{0:T(1024)S(1)}) fusion(f32[2048]{0:T(1024)S(1)} %add_rsqrt_fusion, f32[2048]{0:T(1024)S(1)} %broadcast_multiply_fusion, bf16[2048,768]{1,0:T(8,128)(2,1)S(1)} %copy-done.12, f32[768]{0:T(1024)S(1)} %copy-done.46, ...), kind=kOutput, calls=%fused_computation.166 | convolution fusion | flops 2438722560 | bytes 16943104 | tf_op jit(solution)/shard_map/dot_general | solution.py:368
  335.3 2.7 select_convert_fusion.1
  338.0 2.6 select_convert_fusion
  342.9 6.4 %add_convert_fusion.2 = bf16[2048,768]{1,0:T(8,128)(2,1)} fusion(f32[2048,768]{1,0:T(8,128)} %fusion.56, bf16[2048,384]{1,0:T(8,128)(2,1)S(1)} %get-tuple-element.29, bf16[384,768]{1,0:T(8,128)(2,1)S(1)} %bitcast.148), kind=kOutput, calls=%fused_computation.16 | convolution fusion | flops 1211105280 | bytes 11599872 | tf_op jit(solution)/shard_map/dot_general | solution.py:364
  350.7 1.9 add_convert_fusion.5
  352.6 2.1 copy.154
  361.8 2.8 add_convert_fusion.3
  366.8 2.3 add_convert_fusion.8
  369.1 1.8 collective-permute-done.15
  374.2 2.2 add_convert_fusion.11
  380.1 9.6 %collective-permute-done.30 = bf16[256,768]{1,0:T(8,128)(2,1)S(1)} collective-permute-done((bf16[256,768]{1,0:T(8,128)(2,1)S(1)}, bf16[256,768]{1,0:T(8,128)(2,1)S(1)}, u32[]{:S(2)}, u32[]{:S(2)}) %collective-permute-start.30) | collective-permute-done | bytes 393248 | tf_op jit(solution)/shard_map/ppermute | solution.py:559
  393.2 4.9 %collective-permute-done.16 = bf16[256,768]{1,0:T(8,128)(2,1)S(1)} collective-permute-done((bf16[256,768]{1,0:T(8,128)(2,1)}, bf16[256,768]{1,0:T(8,128)(2,1)S(1)}, u32[]{:S(2)}, u32[]{:S(2)}) %collective-permute-start.16) | collective-permute-done | bytes 393248 | tf_op jit(solution)/shard_map/ppermute | solution.py:559
  402.7 2.6 collective-permute-done.11
  408.1 1.8 convert_reduce_fusion.4
  410.1 10.9 %all_to_all.24 = f32[32,1,288]{2,1,0:T(1,128)S(1)} all-to-all(f32[32,1,288]{2,1,0:T(1,128)S(1)} %copy.143), channel_id=1, replica_groups=mesh['dp'=4,'y'=2,'x'=2,'core'=2] {'dp','y','x','core'}, dimensions={0} | all-to-all | bytes 73728 | tf_op jit(solution)/shard_map/all_to_all | solution.py:735
  421.1 5.3 %all-to-all-start.2 = ((bf16[8,24,288]{2,1,0:T(8,128)(2,1)}), bf16[8,24,288]{2,1,0:T(8,128)(2,1)S(1)}, u32[]{:S(2)}, u32[]{:S(2)}) async-start(bf16[8,24,288]{2,1,0:T(8,128)(2,1)} %bitcast.165), calls=%async_computation.2 | async-start | bytes 294912 | tf_op jit(solution)/shard_map/all_to_all | solution.py:720
  427.7 2.1 all-to-all-done.2
  429.8 5.7 %all-to-all-start.3 = ((bf16[8,24,384]{2,1,0:T(8,128)(2,1)}), bf16[8,24,384]{2,1,0:T(8,128)(2,1)S(1)}, u32[]{:S(2)}, u32[]{:S(2)}) async-start(bf16[8,24,384]{2,1,0:T(8,128)(2,1)} %bitcast.166), calls=%async_computation.5 | async-start | bytes 294912 | tf_op jit(solution)/shard_map/all_to_all | solution.py:694
  441.0 5.0 %collective-permute-start.35 = (bf16[24,768]{1,0:T(8,128)(2,1)S(1)}, bf16[24,768]{1,0:T(8,128)(2,1)S(1)}, u32[]{:S(2)}, u32[]{:S(2)}) collective-permute-start(bf16[24,768]{1,0:T(8,128)(2,1)S(1)} %slice_bitcast_fusion.1), channel_id=1, source_target_pairs={{0,0},{2,8},{4,16},{6,24},{8,2},{10,10},{12,18},{14,26},{16,4},{18... | collective-permute-start | bytes 110600 | tf_op jit(solution)/shard_map/ppermute | solution.py:692
  447.7 2.7 collective-permute-done.35
  (348 shorter events, 91.3 us)
Async XLA Ops:
  9.4 158.2 %collective-permute-start.21 = (bf16[256,768]{1,0:T(8,128)(2,1)}, bf16[256,768]{1,0:T(8,128)(2,1)}, u32[]{:S(2)}, u32[]{:S(2)}) collective-permute-start(bf16[256,768]{1,0:T(8,128)(2,1)} %get-tuple-element.47), channel_id=1, source_target_pairs={{0,4},{4,0},{1,5},{5,1},{2,6},{6,2},{3,7},{7,3},{8,12},{12,8},{9,1... | collective-permute-start | bytes 1179656 | tf_op jit(solution)/shard_map/ppermute | solution.py:559
  9.9 132.1 %collective-permute-start.19 = (bf16[256,768]{1,0:T(8,128)(2,1)}, bf16[256,768]{1,0:T(8,128)(2,1)}, u32[]{:S(2)}, u32[]{:S(2)}) collective-permute-start(bf16[256,768]{1,0:T(8,128)(2,1)} %get-tuple-element.47), channel_id=1, source_target_pairs={{0,2},{2,0},{1,3},{3,1},{4,6},{6,4},{5,7},{7,5},{8,10},{10,8},{9,1... | collective-permute-start | bytes 1179656 | tf_op jit(solution)/shard_map/ppermute | solution.py:559
  10.0 78.6 %collective-permute-start.8 = (bf16[24,768]{1,0:T(8,128)(2,1)}, bf16[24,768]{1,0:T(8,128)(2,1)S(1)}, u32[]{:S(2)}, u32[]{:S(2)}) collective-permute-start(bf16[24,768]{1,0:T(8,128)(2,1)} %param.28), channel_id=1, source_target_pairs={{0,0},{2,8},{4,16},{6,24},{8,2},{10,10},{12,18},{14,26},{16,4},{18... | collective-permute-start | bytes 110600 | tf_op jit(solution)/shard_map/ppermute | solution.py:656
  20.5 47.9 %copy-start.48 = (s32[2,256]{1,0:T(2,128)S(1)}, s32[2,256]{1,0:T(2,128)}, u32[]{:S(2)}) copy-start(s32[2,256]{1,0:T(2,128)} %param.19) | copy-start | bytes 6148
  20.5 47.9 %copy-start.49 = (s32[2,256]{1,0:T(2,128)S(1)}, s32[2,256]{1,0:T(2,128)}, u32[]{:S(2)}) copy-start(s32[2,256]{1,0:T(2,128)} %param.18) | copy-start | bytes 6148
  21.5 86.3 %all-to-all-start = ((bf16[8,24,672]{2,1,0:T(8,128)(2,1)}), bf16[8,24,672]{2,1,0:T(8,128)(2,1)S(1)}, u32[]{:S(2)}, u32[]{:S(2)}) async-start(bf16[8,24,672]{2,1,0:T(8,128)(2,1)} %pad_maximum_fusion.8), calls=%async_computation | async-start | bytes 589824 | tf_op jit(solution)/shard_map/all_to_all | solution.py:617
  25.7 395.4 %reduce-scatter.10.cloned.1.call-start = ((), (), s32[]{:S(2)}) async-start(), calls=%async_computation.9 | async-start | bytes 737280 | tf_op jit(solution)/shard_map/reduce_scatter | solution.py:719
  26.5 117.8 %collective-permute-start = (bf16[256,768]{1,0:T(8,128)(2,1)}, bf16[256,768]{1,0:T(8,128)(2,1)}, u32[]{:S(2)}, u32[]{:S(2)}) collective-permute-start(bf16[256,768]{1,0:T(8,128)(2,1)} %dynamic-slice_bitcast_fusion.2), channel_id=1, source_target_pairs={{0,1},{1,0},{2,3},{3,2},{4,5},{5,4},{6,7},{7,6},{8,9},{9,8},{10,11... | collective-permute-start | bytes 1179656 | tf_op jit(solution)/shard_map/ppermute | solution.py:559
  26.7 113.4 %collective-permute-start.18 = (bf16[256,768]{1,0:T(8,128)(2,1)S(1)}, bf16[256,768]{1,0:T(8,128)(2,1)}, u32[]{:S(2)}, u32[]{:S(2)}) collective-permute-start(bf16[256,768]{1,0:T(8,128)(2,1)S(1)} %dynamic-slice_bitcast_fusion), channel_id=1, source_target_pairs={{0,1},{1,0},{2,3},{3,2},{4,5},{5,4},{6,7},{7,6},{8,9},{9,8},{10,11... | collective-permute-start | bytes 1179656 | tf_op jit(solution)/shard_map/ppermute | solution.py:559
  88.7 58.9 %collective-permute-start.1 = (bf16[256,768]{1,0:T(8,128)(2,1)}, bf16[256,768]{1,0:T(8,128)(2,1)}, u32[]{:S(2)}, u32[]{:S(2)}) collective-permute-start(bf16[256,768]{1,0:T(8,128)(2,1)} %get-tuple-element.49), channel_id=1, source_target_pairs={{0,2},{2,0},{1,3},{3,1},{4,6},{6,4},{5,7},{7,5},{8,10},{10,8},{9,1... | collective-permute-start | bytes 1179656 | tf_op jit(solution)/shard_map/ppermute | solution.py:559
  140.2 9.8 %collective-permute-start.7 = (bf16[768,288]{0,1:T(8,128)(2,1)S(1)}, bf16[768,288]{0,1:T(8,128)(2,1)S(1)}, u32[]{:S(2)}, u32[]{:S(2)}) collective-permute-start(bf16[768,288]{0,1:T(8,128)(2,1)S(1)} %copy.136), channel_id=1, source_target_pairs={{0,1},{1,0},{2,3},{3,2},{4,5},{5,4},{6,7},{7,6},{8,9},{9,8},{10,11... | collective-permute-start | bytes 1327112 | tf_op jit(solution)/shard_map/ppermute | solution.py:559
  142.0 13.7 %collective-permute-start.9 = (bf16[4,120,768]{2,1,0:T(8,128)(2,1)}, bf16[4,120,768]{2,1,0:T(8,128)(2,1)}, u32[]{:S(2)}, u32[]{:S(2)}) collective-permute-start(bf16[4,120,768]{2,1,0:T(8,128)(2,1)} %bitcast.19), channel_id=1, source_target_pairs={{0,1},{1,0},{2,3},{3,2},{4,5},{5,4},{6,7},{7,6},{8,9},{9,8},{10,11... | collective-permute-start | bytes 2211848 | tf_op jit(solution)/shard_map/ppermute | solution.py:559
  144.3 28.6 %collective-permute-start.3 = (bf16[256,768]{1,0:T(8,128)(2,1)}, bf16[256,768]{1,0:T(8,128)(2,1)}, u32[]{:S(2)}, u32[]{:S(2)}) collective-permute-start(bf16[256,768]{1,0:T(8,128)(2,1)} %get-tuple-element.49), channel_id=1, source_target_pairs={{0,4},{4,0},{1,5},{5,1},{2,6},{6,2},{3,7},{7,3},{8,12},{12,8},{9,1... | collective-permute-start | bytes 1179656 | tf_op jit(solution)/shard_map/ppermute | solution.py:559
  147.6 23.7 %collective-permute-start.2 = (bf16[256,768]{1,0:T(8,128)(2,1)}, bf16[256,768]{1,0:T(8,128)(2,1)}, u32[]{:S(2)}, u32[]{:S(2)}) collective-permute-start(bf16[256,768]{1,0:T(8,128)(2,1)} %collective-permute-done), channel_id=1, source_target_pairs={{0,2},{2,0},{1,3},{3,1},{4,6},{6,4},{5,7},{7,5},{8,10},{10,8},{9,1... | collective-permute-start | bytes 1179656 | tf_op jit(solution)/shard_map/ppermute | solution.py:559
  149.9 18.8 %collective-permute-start.22 = (bf16[256,768]{1,0:T(8,128)(2,1)}, bf16[256,768]{1,0:T(8,128)(2,1)}, u32[]{:S(2)}, u32[]{:S(2)}) collective-permute-start(bf16[256,768]{1,0:T(8,128)(2,1)} %collective-permute-done.18), channel_id=1, source_target_pairs={{0,4},{4,0},{1,5},{5,1},{2,6},{6,2},{3,7},{7,3},{8,12},{12,8},{9,1... | collective-permute-start | bytes 1179656 | tf_op jit(solution)/shard_map/ppermute | solution.py:559
  155.7 11.3 %collective-permute-start.20 = (bf16[256,768]{1,0:T(8,128)(2,1)}, bf16[256,768]{1,0:T(8,128)(2,1)S(1)}, u32[]{:S(2)}, u32[]{:S(2)}) collective-permute-start(bf16[256,768]{1,0:T(8,128)(2,1)} %collective-permute-done.18), channel_id=1, source_target_pairs={{0,2},{2,0},{1,3},{3,1},{4,6},{6,4},{5,7},{7,5},{8,10},{10,8},{9,1... | collective-permute-start | bytes 1179656 | tf_op jit(solution)/shard_map/ppermute | solution.py:559
  158.0 121.1 %copy-start.27 = (bf16[2,4,96,768]{3,2,1,0:T(8,128)(2,1)}, bf16[2,4,96,768]{3,2,1,0:T(8,128)(2,1)S(1)}, u32[]{:S(2)}) copy-start(bf16[2,4,96,768]{3,2,1,0:T(8,128)(2,1)S(1)} %copy.141) | copy-start | bytes 3538948
  167.0 12.3 %collective-permute-start.4 = (bf16[256,768]{1,0:T(8,128)(2,1)}, bf16[256,768]{1,0:T(8,128)(2,1)S(1)}, u32[]{:S(2)}, u32[]{:S(2)}) collective-permute-start(bf16[256,768]{1,0:T(8,128)(2,1)} %collective-permute-done), channel_id=1, source_target_pairs={{0,4},{4,0},{1,5},{5,1},{2,6},{6,2},{3,7},{7,3},{8,12},{12,8},{9,1... | collective-permute-start | bytes 1179656 | tf_op jit(solution)/shard_map/ppermute | solution.py:559
  167.6 26.6 %collective-permute-start.10 = (bf16[768,384]{1,0:T(8,128)(2,1)S(1)}, bf16[768,384]{1,0:T(8,128)(2,1)S(1)}, u32[]{:S(2)}, u32[]{:S(2)}) collective-permute-start(bf16[768,384]{1,0:T(8,128)(2,1)S(1)} %all_gather.31), channel_id=1, source_target_pairs={{0,1},{1,0},{2,3},{3,2},{4,5},{5,4},{6,7},{7,6},{8,9},{9,8},{10,11... | collective-permute-start | bytes 1769480 | tf_op jit(solution)/shard_map/ppermute | solution.py:559
  168.7 19.0 %collective-permute-start.23 = (bf16[256,768]{1,0:T(8,128)(2,1)}, bf16[256,768]{1,0:T(8,128)(2,1)S(1)}, u32[]{:S(2)}, u32[]{:S(2)}) collective-permute-start(bf16[256,768]{1,0:T(8,128)(2,1)} %collective-permute-done.19), channel_id=1, source_target_pairs={{0,4},{4,0},{1,5},{5,1},{2,6},{6,2},{3,7},{7,3},{8,12},{12,8},{9,1... | collective-permute-start | bytes 1179656 | tf_op jit(solution)/shard_map/ppermute | solution.py:559
  171.3 22.8 %collective-permute-start.5 = (bf16[256,768]{1,0:T(8,128)(2,1)}, bf16[256,768]{1,0:T(8,128)(2,1)S(1)}, u32[]{:S(2)}, u32[]{:S(2)}) collective-permute-start(bf16[256,768]{1,0:T(8,128)(2,1)} %collective-permute-done.1), channel_id=1, source_target_pairs={{0,4},{4,0},{1,5},{5,1},{2,6},{6,2},{3,7},{7,3},{8,12},{12,8},{9,1... | collective-permute-start | bytes 1179656 | tf_op jit(solution)/shard_map/ppermute | solution.py:559
  172.9 21.9 %collective-permute-start.24 = (bf16[256,768]{1,0:T(8,128)(2,1)}, bf16[256,768]{1,0:T(8,128)(2,1)S(1)}, u32[]{:S(2)}, u32[]{:S(2)}) collective-permute-start(bf16[256,768]{1,0:T(8,128)(2,1)} %collective-permute-done.22), channel_id=1, source_target_pairs={{0,2},{2,0},{1,3},{3,1},{4,6},{6,4},{5,7},{7,5},{8,10},{10,8},{9,1... | collective-permute-start | bytes 1179656 | tf_op jit(solution)/shard_map/ppermute | solution.py:559
  179.2 15.1 %collective-permute-start.6 = (bf16[256,768]{1,0:T(8,128)(2,1)S(1)}, bf16[256,768]{1,0:T(8,128)(2,1)S(1)}, u32[]{:S(2)}, u32[]{:S(2)}) collective-permute-start(bf16[256,768]{1,0:T(8,128)(2,1)S(1)} %collective-permute-done.4), channel_id=1, source_target_pairs={{0,2},{2,0},{1,3},{3,1},{4,6},{6,4},{5,7},{7,5},{8,10},{10,8},{9,1... | collective-permute-start | bytes 1179656 | tf_op jit(solution)/shard_map/ppermute | solution.py:559
  194.3 82.2 %copy-start.29 = (bf16[768,384]{1,0:T(8,128)(2,1)}, bf16[768,384]{1,0:T(8,128)(2,1)S(1)}, u32[]{:S(2)}) copy-start(bf16[768,384]{1,0:T(8,128)(2,1)S(1)} %get-tuple-element.71) | copy-start | bytes 1769476
  194.3 82.2 %copy-start.31 = (bf16[768,384]{1,0:T(8,128)(2,1)}, bf16[768,384]{1,0:T(8,128)(2,1)S(1)}, u32[]{:S(2)}) copy-start(bf16[768,384]{1,0:T(8,128)(2,1)S(1)} %get-tuple-element.72) | copy-start | bytes 1769476
  313.5 44.5 %collective-permute-start.34 = (bf16[4,24,768]{2,1,0:T(8,128)(2,1)S(1)}, bf16[4,24,768]{2,1,0:T(8,128)(2,1)S(1)}, u32[]{:S(2)}, u32[]{:S(2)}) collective-permute-start(bf16[4,24,768]{2,1,0:T(8,128)(2,1)S(1)} %fusion.39), channel_id=1, source_target_pairs={{0,1},{1,0},{2,3},{3,2},{4,5},{5,4},{6,7},{7,6},{8,9},{9,8},{10,11... | collective-permute-start | bytes 442376 | tf_op jit(solution)/shard_map/ppermute | solution.py:559
  323.5 25.8 %collective-permute-start.32 = (bf16[768,288]{0,1:T(8,128)(2,1)}, bf16[768,288]{0,1:T(8,128)(2,1)}, u32[]{:S(2)}, u32[]{:S(2)}) collective-permute-start(bf16[768,288]{0,1:T(8,128)(2,1)} %select_convert_fusion.2), channel_id=1, source_target_pairs={{0,1},{1,0},{2,3},{3,2},{4,5},{5,4},{6,7},{7,6},{8,9},{9,8},{10,11... | collective-permute-start | bytes 1327112 | tf_op jit(solution)/shard_map/ppermute | solution.py:559
  340.6 20.0 %collective-permute-start.36 = (bf16[768,384]{1,0:T(8,128)(2,1)}, bf16[768,384]{1,0:T(8,128)(2,1)}, u32[]{:S(2)}, u32[]{:S(2)}) collective-permute-start(bf16[768,384]{1,0:T(8,128)(2,1)} %select_convert_fusion), channel_id=1, source_target_pairs={{0,1},{1,0},{2,3},{3,2},{4,5},{5,4},{6,7},{7,6},{8,9},{9,8},{10,11... | collective-permute-start | bytes 1769480 | tf_op jit(solution)/shard_map/ppermute | solution.py:559
  341.1 35.3 %collective-permute-start.33 = (bf16[384,768]{1,0:T(8,128)(2,1)}, bf16[384,768]{1,0:T(8,128)(2,1)}, u32[]{:S(2)}, u32[]{:S(2)}) collective-permute-start(bf16[384,768]{1,0:T(8,128)(2,1)} %select_convert_fusion.1), channel_id=1, source_target_pairs={{0,1},{1,0},{2,3},{3,2},{4,5},{5,4},{6,7},{7,6},{8,9},{9,8},{10,11... | collective-permute-start | bytes 1769480 | tf_op jit(solution)/shard_map/ppermute | solution.py:559
  342.3 22.4 %collective-permute-start.29 = (bf16[256,768]{1,0:T(8,128)(2,1)}, bf16[256,768]{1,0:T(8,128)(2,1)}, u32[]{:S(2)}, u32[]{:S(2)}) collective-permute-start(bf16[256,768]{1,0:T(8,128)(2,1)} %get-tuple-element.58), channel_id=1, source_target_pairs={{0,2},{2,0},{1,3},{3,1},{4,6},{6,4},{5,7},{7,5},{8,10},{10,8},{9,1... | collective-permute-start | bytes 1179656 | tf_op jit(solution)/shard_map/ppermute | solution.py:559
  349.2 16.4 %collective-permute-start.26 = (bf16[256,768]{1,0:T(8,128)(2,1)}, bf16[256,768]{1,0:T(8,128)(2,1)}, u32[]{:S(2)}, u32[]{:S(2)}) collective-permute-start(bf16[256,768]{1,0:T(8,128)(2,1)} %get-tuple-element.60), channel_id=1, source_target_pairs={{0,4},{4,0},{1,5},{5,1},{2,6},{6,2},{3,7},{7,3},{8,12},{12,8},{9,1... | collective-permute-start | bytes 1179656 | tf_op jit(solution)/shard_map/ppermute | solution.py:559
  354.7 75.1 %reduce-scatter.8.cloned.1.call-start = ((), (), s32[]{:S(2)}) async-start(), calls=%async_computation.8 | async-start | bytes 737280 | tf_op jit(solution)/shard_map/reduce_scatter | solution.py:693
  358.6 12.3 %collective-permute-start.15 = (bf16[256,768]{1,0:T(8,128)(2,1)}, bf16[256,768]{1,0:T(8,128)(2,1)}, u32[]{:S(2)}, u32[]{:S(2)}) collective-permute-start(bf16[256,768]{1,0:T(8,128)(2,1)} %get-tuple-element.64), channel_id=1, source_target_pairs={{0,2},{2,0},{1,3},{3,1},{4,6},{6,4},{5,7},{7,5},{8,10},{10,8},{9,1... | collective-permute-start | bytes 1179656 | tf_op jit(solution)/shard_map/ppermute | solution.py:559
  360.6 12.4 %collective-permute-start.12 = (bf16[256,768]{1,0:T(8,128)(2,1)}, bf16[256,768]{1,0:T(8,128)(2,1)}, u32[]{:S(2)}, u32[]{:S(2)}) collective-permute-start(bf16[256,768]{1,0:T(8,128)(2,1)} %get-tuple-element.66), channel_id=1, source_target_pairs={{0,4},{4,0},{1,5},{5,1},{2,6},{6,2},{3,7},{7,3},{8,12},{12,8},{9,1... | collective-permute-start | bytes 1179656 | tf_op jit(solution)/shard_map/ppermute | solution.py:559
  364.6 75.6 %reduce-scatter.6.cloned.1.call-start = ((), (), s32[]{:S(2)}) async-start(), calls=%async_computation.7 | async-start | bytes 921600 | tf_op jit(solution)/shard_map/reduce_scatter | solution.py:690
  364.7 35.9 %collective-permute-start.25 = (bf16[256,768]{1,0:T(8,128)(2,1)}, bf16[256,768]{1,0:T(8,128)(2,1)}, u32[]{:S(2)}, u32[]{:S(2)}) collective-permute-start(bf16[256,768]{1,0:T(8,128)(2,1)} %get-tuple-element.57), channel_id=1, source_target_pairs={{0,4},{4,0},{1,5},{5,1},{2,6},{6,2},{3,7},{7,3},{8,12},{12,8},{9,1... | collective-permute-start | bytes 1179656 | tf_op jit(solution)/shard_map/ppermute | solution.py:559
  365.6 13.6 %collective-permute-start.28 = (bf16[256,768]{1,0:T(8,128)(2,1)}, bf16[256,768]{1,0:T(8,128)(2,1)S(1)}, u32[]{:S(2)}, u32[]{:S(2)}) collective-permute-start(bf16[256,768]{1,0:T(8,128)(2,1)} %get-tuple-element.59), channel_id=1, source_target_pairs={{0,2},{2,0},{1,3},{3,1},{4,6},{6,4},{5,7},{7,5},{8,10},{10,8},{9,1... | collective-permute-start | bytes 1179656 | tf_op jit(solution)/shard_map/ppermute | solution.py:559
  370.9 21.1 %collective-permute-start.14 = (bf16[256,768]{1,0:T(8,128)(2,1)}, bf16[256,768]{1,0:T(8,128)(2,1)}, u32[]{:S(2)}, u32[]{:S(2)}) collective-permute-start(bf16[256,768]{1,0:T(8,128)(2,1)} %get-tuple-element.65), channel_id=1, source_target_pairs={{0,2},{2,0},{1,3},{3,1},{4,6},{6,4},{5,7},{7,5},{8,10},{10,8},{9,1... | collective-permute-start | bytes 1179656 | tf_op jit(solution)/shard_map/ppermute | solution.py:559
  373.0 16.7 %collective-permute-start.30 = (bf16[256,768]{1,0:T(8,128)(2,1)S(1)}, bf16[256,768]{1,0:T(8,128)(2,1)S(1)}, u32[]{:S(2)}, u32[]{:S(2)}) collective-permute-start(bf16[256,768]{1,0:T(8,128)(2,1)S(1)} %get-tuple-element.62), channel_id=1, source_target_pairs={{0,4},{4,0},{1,5},{5,1},{2,6},{6,2},{3,7},{7,3},{8,12},{12,8},{9,1... | collective-permute-start | bytes 1179656 | tf_op jit(solution)/shard_map/ppermute | solution.py:559
  376.4 24.3 %collective-permute-start.27 = (bf16[256,768]{1,0:T(8,128)(2,1)}, bf16[256,768]{1,0:T(8,128)(2,1)S(1)}, u32[]{:S(2)}, u32[]{:S(2)}) collective-permute-start(bf16[256,768]{1,0:T(8,128)(2,1)} %get-tuple-element.61), channel_id=1, source_target_pairs={{0,2},{2,0},{1,3},{3,1},{4,6},{6,4},{5,7},{7,5},{8,10},{10,8},{9,1... | collective-permute-start | bytes 1179656 | tf_op jit(solution)/shard_map/ppermute | solution.py:559
  379.2 18.9 %collective-permute-start.16 = (bf16[256,768]{1,0:T(8,128)(2,1)}, bf16[256,768]{1,0:T(8,128)(2,1)S(1)}, u32[]{:S(2)}, u32[]{:S(2)}) collective-permute-start(bf16[256,768]{1,0:T(8,128)(2,1)} %get-tuple-element.68), channel_id=1, source_target_pairs={{0,4},{4,0},{1,5},{5,1},{2,6},{6,2},{3,7},{7,3},{8,12},{12,8},{9,1... | collective-permute-start | bytes 1179656 | tf_op jit(solution)/shard_map/ppermute | solution.py:559
  390.9 9.8 %collective-permute-start.31 = (bf16[256,768]{1,0:T(8,128)(2,1)S(1)}, bf16[256,768]{1,0:T(8,128)(2,1)S(1)}, u32[]{:S(2)}, u32[]{:S(2)}) collective-permute-start(bf16[256,768]{1,0:T(8,128)(2,1)S(1)} %add_convert_fusion.6), channel_id=1, source_target_pairs={{0,1},{1,0},{2,3},{3,2},{4,5},{5,4},{6,7},{7,6},{8,9},{9,8},{10,11... | collective-permute-start | bytes 1179656 | tf_op jit(solution)/shard_map/ppermute | solution.py:559
  392.0 13.3 %collective-permute-start.11 = (bf16[256,768]{1,0:T(8,128)(2,1)S(1)}, bf16[256,768]{1,0:T(8,128)(2,1)S(1)}, u32[]{:S(2)}, u32[]{:S(2)}) collective-permute-start(bf16[256,768]{1,0:T(8,128)(2,1)S(1)} %copy-done.33), channel_id=1, source_target_pairs={{0,4},{4,0},{1,5},{5,1},{2,6},{6,2},{3,7},{7,3},{8,12},{12,8},{9,1... | collective-permute-start | bytes 1179656 | tf_op jit(solution)/shard_map/ppermute | solution.py:559
  398.1 8.7 %collective-permute-start.13 = (bf16[256,768]{1,0:T(8,128)(2,1)S(1)}, bf16[256,768]{1,0:T(8,128)(2,1)S(1)}, u32[]{:S(2)}, u32[]{:S(2)}) collective-permute-start(bf16[256,768]{1,0:T(8,128)(2,1)S(1)} %copy-done.34), channel_id=1, source_target_pairs={{0,2},{2,0},{1,3},{3,1},{4,6},{6,4},{5,7},{7,5},{8,10},{10,8},{9,1... | collective-permute-start | bytes 1179656 | tf_op jit(solution)/shard_map/ppermute | solution.py:559
  400.6 6.2 %collective-permute-start.17 = (bf16[256,768]{1,0:T(8,128)(2,1)S(1)}, bf16[256,768]{1,0:T(8,128)(2,1)S(1)}, u32[]{:S(2)}, u32[]{:S(2)}) collective-permute-start(bf16[256,768]{1,0:T(8,128)(2,1)S(1)} %add_convert_fusion.9), channel_id=1, source_target_pairs={{0,1},{1,0},{2,3},{3,2},{4,5},{5,4},{6,7},{7,6},{8,9},{9,8},{10,11... | collective-permute-start | bytes 1179656 | tf_op jit(solution)/shard_map/ppermute | solution.py:559
  421.1 8.7 %all-to-all-start.2 = ((bf16[8,24,288]{2,1,0:T(8,128)(2,1)}), bf16[8,24,288]{2,1,0:T(8,128)(2,1)S(1)}, u32[]{:S(2)}, u32[]{:S(2)}) async-start(bf16[8,24,288]{2,1,0:T(8,128)(2,1)} %bitcast.165), calls=%async_computation.2 | async-start | bytes 294912 | tf_op jit(solution)/shard_map/all_to_all | solution.py:720
  429.8 9.0 %all-to-all-start.3 = ((bf16[8,24,384]{2,1,0:T(8,128)(2,1)}), bf16[8,24,384]{2,1,0:T(8,128)(2,1)S(1)}, u32[]{:S(2)}, u32[]{:S(2)}) async-start(bf16[8,24,384]{2,1,0:T(8,128)(2,1)} %bitcast.166), calls=%async_computation.5 | async-start | bytes 294912 | tf_op jit(solution)/shard_map/all_to_all | solution.py:694
  441.0 9.4 %collective-permute-start.35 = (bf16[24,768]{1,0:T(8,128)(2,1)S(1)}, bf16[24,768]{1,0:T(8,128)(2,1)S(1)}, u32[]{:S(2)}, u32[]{:S(2)}) collective-permute-start(bf16[24,768]{1,0:T(8,128)(2,1)S(1)} %slice_bitcast_fusion.1), channel_id=1, source_target_pairs={{0,0},{2,8},{4,16},{6,24},{8,2},{10,10},{12,18},{14,26},{16,4},{18... | collective-permute-start | bytes 110600 | tf_op jit(solution)/shard_map/ppermute | solution.py:692
  (59 other events, 559.0 us)
Sparse Core Ops, SparseCore 0:
  354.8 22.0 reduce-scatter.9
  379.1 20.3 reduce-scatter.7
  401.8 21.6 reduce-scatter.5
